TPU v7x, 128 devices: a whole 4x4x4 slice. The times are simulated.
128 devices in a mesh: dp: 8 (over z, core), seq: 16 (over y, x).
Axes of the slice: x: 4, y: 4, z: 4, core: 2. Of those that a mesh axis runs over, the one named last changes fastest.
Arguments:
- query_heads: bfloat16 [8, 6144, 4096], P('dp', 'seq'), may hold values from -6 to 6
- key_heads: bfloat16 [8, 6144, 4096], P('dp', 'seq'), may hold values from -6 to 6
- value_heads: bfloat16 [8, 6144, 4096], P('dp', 'seq'), may hold values from -6 to 6
- output_grad: bfloat16 [8, 6144, 4096], P('dp', 'seq'), may hold values from -6 to 6
- layer_input: bfloat16 [8, 6144, 6144], P('dp', 'seq'), may hold values from -6 to 6
- gate_weight: bfloat16 [6144, 32], replicated, may hold values from -0.078125 to 0.078125
- decay_rate: float32 [8, 32, 6144], P('dp', None, 'seq'), may hold values from 0 to 0.3, as said below
Outputs:
- query_grad: bfloat16 [8, 6144, 4096], P('dp', 'seq')
- key_grad: bfloat16 [8, 6144, 4096], P('dp', 'seq')
- value_grad: bfloat16 [8, 6144, 4096], P('dp', 'seq')
- gate_weight_grad: float32 [32, 6144], P(None, 'seq')
Inputs may be any that keep to these rules, and one draw needn't show every extreme that they name: `decay_rate`: positive rates.
All inputs are finite; a program needn't handle non-finite values.
Results may differ from a plain program's by a relative error of at most 0.009.
Values sent between devices are 32-bit elements; how exact they have to be, the bound alone decides.
No kernel may reach another device: no remote copies, remote signals or barrier semaphores. Data moves between devices by JAX's collectives and lax.ppermute only.
A program may use at most 256 MiB of HBM per device.

v0:
```python
import jax
import jax.numpy as jnp
from jax import lax
from jax.sharding import PartitionSpec as P


def carried_in(part, axis, combine, identity, reverse):
    count = lax.axis_size(axis)
    place = lax.axis_index(axis)
    ahead = count - 1 - place if reverse else place
    gathered = jax.tree.map(lambda a: lax.all_gather(a, axis), part)
    state = jax.tree.map(lambda a, e: jnp.zeros_like(a) + jnp.asarray(e, a.dtype), part, identity)

    def one(step, state):
        source = count - 1 - step if reverse else step
        return combine(
            state, jax.tree.map(lambda a: lax.dynamic_index_in_dim(a, source, 0, False), gathered)
        )

    return lax.fori_loop(0, ahead, one, state)


def combine(earlier, later):
    return (earlier[0] * later[0], later[0][:, None, None] * earlier[1] + later[1])


def add_tail(earlier, later):
    return earlier + later


def local(query_heads, key_heads, value_heads, output_grad, layer_input, gate_weight, decay_rate):
    block_len = query_heads.shape[1]
    head_count = decay_rate.shape[1]
    head_dim = query_heads.shape[2] // head_count
    scale_factor = 1.0 / head_dim
    query_rows = query_heads[0].reshape(block_len, head_count, head_dim)
    key_rows = key_heads[0].reshape(block_len, head_count, head_dim)
    value_rows = value_heads[0].reshape(block_len, head_count, head_dim)
    grad_rows = output_grad[0].reshape(block_len, head_count, head_dim)
    gate_open = jax.nn.sigmoid(
        jnp.dot(layer_input[0], gate_weight, preferred_element_type=jnp.float32).T
    )
    log_gate = -2.0 * decay_rate[0] * gate_open
    token_position = jnp.arange(block_len)
    upper_ones = (token_position[:, None] <= token_position[None, :]).astype(jnp.float32)
    running = jnp.dot(
        log_gate, upper_ones, precision=lax.Precision.HIGHEST, preferred_element_type=jnp.float32
    )
    block_total = running[:, -1]
    causal = (token_position[:, None] >= token_position[None, :])[None]
    log_gap = jnp.where(causal, running[:, :, None] - running[:, None, :], 0.0)
    decay_table = jnp.where(causal, jnp.exp(log_gap), 0.0) * scale_factor
    scores = jnp.einsum("thd,shd->hts", query_rows, key_rows, preferred_element_type=jnp.float32)
    weighted = (scores * decay_table).astype(jnp.bfloat16)
    grad_scores = jnp.einsum(
        "thd,shd->hts", grad_rows, value_rows, preferred_element_type=jnp.float32
    )
    mixing = (grad_scores * decay_table).astype(jnp.bfloat16)
    query_local = jnp.einsum("hts,shd->thd", mixing, key_rows, preferred_element_type=jnp.float32)
    key_local = jnp.einsum("hts,thd->shd", mixing, query_rows, preferred_element_type=jnp.float32)
    value_local = jnp.einsum(
        "hts,thd->shd", weighted, grad_rows, preferred_element_type=jnp.float32
    )
    to_end = jnp.exp(block_total[:, None] - running).T[:, :, None]
    from_start = jnp.exp(running).T[:, :, None]
    key_faded = (key_rows * to_end).astype(jnp.bfloat16)
    query_faded = (query_rows * from_start).astype(jnp.bfloat16)
    states = jnp.einsum("thd,the->hde", key_faded, value_rows, preferred_element_type=jnp.float32)
    grad_state = jnp.einsum(
        "thd,the->hde", query_faded, grad_rows, preferred_element_type=jnp.float32
    )
    fading = jnp.exp(block_total)
    unit_fade = jnp.ones_like(fading)
    zero_state = jnp.zeros_like(states)
    prior_state = carried_in((fading, states), "seq", combine, (unit_fade, zero_state), False)[1]
    later_state = carried_in((fading, grad_state), "seq", combine, (unit_fade, zero_state), True)[1]
    prior_low = prior_state.astype(jnp.bfloat16)
    later_low = later_state.astype(jnp.bfloat16)
    query_full = query_local + from_start * scale_factor * jnp.einsum(
        "the,hde->thd", grad_rows, prior_low, preferred_element_type=jnp.float32
    )
    key_full = key_local + to_end * scale_factor * jnp.einsum(
        "the,hde->thd", value_rows, later_low, preferred_element_type=jnp.float32
    )
    value_full = value_local + to_end * scale_factor * jnp.einsum(
        "thd,hde->the", key_rows, later_low, preferred_element_type=jnp.float32
    )
    gate_push = jnp.sum(query_rows * query_full - key_rows * key_full, axis=2).T
    block_sums = jnp.sum(gate_push, axis=1)
    tail_sum = carried_in(block_sums, "seq", add_tail, jnp.zeros_like(block_sums), True)
    lower_ones = (token_position[:, None] >= token_position[None, :]).astype(jnp.float32)
    suffix_sum = jnp.dot(
        gate_push, lower_ones, precision=lax.Precision.HIGHEST, preferred_element_type=jnp.float32
    )
    gate_grad = suffix_sum + tail_sum[:, None]
    logit_grad = (gate_grad * log_gate * (1.0 - gate_open)).astype(jnp.bfloat16)
    gate_term = jnp.dot(logit_grad, layer_input[0], preferred_element_type=jnp.float32)
    token_count = block_len * lax.axis_size("seq") * lax.axis_size("dp")
    summed = lax.psum(gate_term, ("dp", "seq"))
    col_count = summed.shape[1] // lax.axis_size("seq")
    own_columns = lax.dynamic_slice_in_dim(summed, lax.axis_index("seq") * col_count, col_count, 1)
    weight_grad = own_columns / token_count
    return (
        query_full.reshape(1, block_len, -1).astype(jnp.bfloat16),
        key_full.reshape(1, block_len, -1).astype(jnp.bfloat16),
        value_full.reshape(1, block_len, -1).astype(jnp.bfloat16),
        weight_grad,
    )


def solution(mesh):
    placed = (
        P("dp", "seq", None),
        P("dp", "seq", None),
        P("dp", "seq", None),
        P("dp", "seq", None),
        P("dp", "seq", None),
        P(),
        P("dp", None, "seq"),
    )
    return jax.shard_map(
        local,
        mesh=mesh,
        in_specs=placed,
        out_specs=(
            P("dp", "seq", None),
            P("dp", "seq", None),
            P("dp", "seq", None),
            P(None, "seq"),
        ),
        check_vma=False,
    )
```

profile of v0, /device:TPU:1, one launch (start us, length us, event | category | flops | bytes accessed | tf_op | source)
XLA Modules:
  0.0 681.3 jit_solution(13199853477543474538)
XLA Ops:
  7.2 0.9 copy-done
  8.2 3.8 fusion.36
  12.0 0.2 fusion.41
  12.7 3.4 copy.41
  16.2 3.9 copy.60
  20.1 1.7 copy-done.6
  21.7 4.5 fusion.17
  26.3 4.7 copy.44
  31.0 4.6 copy.59
  35.7 5.6 fusion.15
  41.4 0.6 dynamic-slice
  42.5 0.2 dynamic-update-slice
  42.7 35.5 %all-reduce = f32[512]{0:T(512)S(1)} all-reduce(f32[512]{0:T(512)S(1)} %dynamic-update-slice), channel_id=2, replica_groups=mesh['dp'=8,'seq'=16] {'seq'}, use_global_device_ids=true, to_apply=%add | all-reduce | flops 512 | bytes 4096
  78.3 16.3 %multiply_convert_fusion.1 = bf16[32,384,384]{2,1,0:T(8,128)(2,1)} fusion(f32[32,384]{1,0:T(8,128)S(1)} %fusion.41, pred[384,384]{1,0:T(8,128)(4,1)S(1)} %iota_compare_fusion.1, bf16[384,32,128]{0,2,1:T(8,128)(2,1)} %bitcast.97, bf16[384,32,128]{2,1,0:T(8,128)(2,1)} %bitcast.104), kind=kOutput, calls=%fused_computation.6 | convolution fusion | flops 1236271104 | bytes 15925248 | tf_op jit(solution)/shard_map/thd,shd->hts/dot_general | solution.py:55
  94.6 9.3 %fusion.50 = f32[32,384,128]{1,2,0:T(8,128)} fusion(bf16[32,384,384]{2,1,0:T(8,128)(2,1)} %multiply_convert_fusion.1, bf16[384,32,128]{0,2,1:T(8,128)(2,1)S(1)} %bitcast.92), kind=kOutput, calls=%fused_computation.65 | convolution fusion | flops 1207959552 | bytes 18874368 | tf_op jit(solution)/shard_map/hts,shd->thd/dot_general | solution.py:59
  103.9 12.3 %fusion = f32[32,384,128]{1,2,0:T(8,128)} fusion(bf16[384,32,128]{0,2,1:T(8,128)(2,1)} %bitcast.98, f32[32,384]{1,0:T(8,128)S(1)} %fusion.41, pred[384,384]{1,0:T(8,128)(4,1)S(1)} %iota_compare_fusion.1, bf16[384,32,128]{0,2,1:T(8,128)(2,1)} %bitcast.101, bf16[384,32,128]{0,2,1:T(8,128)(2,1)S(1)} %bitcast.93), kind=kOutput, calls=%fused_computation.8 | convolution fusion | flops 2444230656 | bytes 15925248 | tf_op jit(solution)/shard_map/hts,thd->shd/dot_general | solution.py:61
  116.2 110.7 %all-gather.7.cloned.1.call-done = f32[512,128,128]{2,1,0:T(8,128)} async-done(((f32[32,128,128]{2,1,0:T(8,128)}), f32[512,128,128]{2,1,0:T(8,128)}) %all-gather.7.cloned.1.call-update) | async-done | bytes 33554448 | tf_op jit(solution)/shard_map/all_gather | solution.py:11
  227.1 198.6 %all-gather.9.cloned.1.call-done = f32[512,128,128]{2,1,0:T(8,128)} async-done(((f32[32,128,128]{2,1,0:T(8,128)}), f32[512,128,128]{2,1,0:T(8,128)}) %all-gather.9.cloned.1.call-update) | async-done | bytes 33554448 | tf_op jit(solution)/shard_map/all_gather | solution.py:11
  425.7 0.2 broadcast_in_dim.43.clone.1
  426.0 30.6 %while.39 = (s32[]{:T(128)}, f32[32,128,128]{2,1,0:T(8,128)S(1)}, s32[]{:T(128)}, f32[16,32]{1,0:T(8,128)S(1)}, f32[16,32,128,128]{3,2,1,0:T(8,128)}, /*index=5*/s32[]{:T(128)}, s32[]{:T(128)}, s32[]{:T(128)}, s32[]{:T(128)}) while((s32[]{:T(128)}, f32[32,128,128]{2,1,0:T(8,128)S(1)}, s32[]{:T(128)}, f32[16,32]{1,0:T(8,128)S(1)}, ...), condition=%wide.region_3.4_spmd, body=%wide.region_2.3_spmd.sunk | while | flops 1048582 | bytes 6291995 | solution.py:20
  426.2 2.0 bitcast_add_fusion.7
  428.2 2.0 bitcast_add_fusion.7
  430.3 2.0 bitcast_add_fusion.7
  432.3 2.0 bitcast_add_fusion.7
  434.3 2.0 bitcast_add_fusion.7
  436.3 2.0 bitcast_add_fusion.7
  438.4 2.0 bitcast_add_fusion.7
  440.4 2.0 bitcast_add_fusion.7
  442.4 2.0 bitcast_add_fusion.7
  444.4 2.0 bitcast_add_fusion.7
  446.4 2.0 bitcast_add_fusion.7
  448.5 2.0 bitcast_add_fusion.7
  450.5 2.0 bitcast_add_fusion.7
  452.5 2.0 bitcast_add_fusion.7
  454.5 2.0 bitcast_add_fusion.7
  456.5 7.8 %fusion.21 = f32[32,128,384]{2,1,0:T(8,128)} fusion(bf16[384,32,128]{2,1,0:T(8,128)(2,1)} %bitcast.105, f32[32,128,128]{2,1,0:T(8,128)S(1)} %get-tuple-element.189), kind=kOutput, calls=%fused_computation.33 | convolution fusion | flops 403177472 | bytes 11534336 | tf_op jit(solution)/shard_map/the,hde->thd/dot_general | solution.py:82
  464.3 6.6 fusion.8
  470.9 17.3 %fusion.48 = (f32[32]{0:T(128)S(1)}, f32[384,32]{0,1:T(8,128)S(1)}, bf16[384,32,128]{0,2,1:T(8,128)(2,1)}, bf16[384,32,128]{0,2,1:T(8,128)(2,1)}) fusion(bf16[384,32,128]{0,2,1:T(8,128)(2,1)} %bitcast.94, f32[384,32,128]{0,2,1:T(8,128)} %fusion.8, bf16[384,32,128]{0,2,1:T(8,128)(2,1)} %bitcast.102, f32[32,128,384]{2,1,0:T(8,128)} %fusion.21, ...), kind=kOutput, calls=%fused_computation.63 | convolution fusion | flops 1225248768 | bytes 34701440 | tf_op jit(solution)/shard_map/hts,thd->shd/dot_general | solution.py:60
  488.4 28.5 %all-reduce.1 = f32[512]{0:T(512)S(1)} all-reduce(f32[512]{0:T(512)S(1)} %dynamic-update-slice.1), channel_id=5, replica_groups=mesh['dp'=8,'seq'=16] {'seq'}, use_global_device_ids=true, to_apply=%add.1 | all-reduce | flops 512 | bytes 4096
  516.9 0.6 while.40
  517.5 0.3 fusion.39
  517.8 4.2 fusion.11
  522.0 6.5 fusion.6
  528.4 4.6 copy.54
  533.1 4.8 copy.52
  537.8 2.8 copy.53
  540.7 132.6 %all-reduce.4.cloned.1.call-done = f32[32,6144]{1,0:T(8,128)} async-done(((f32[32,6144]{1,0:T(8,128)}), f32[32,6144]{1,0:T(8,128)}) %all-reduce.4.cloned.1.call-update) | async-done | bytes 786448 | tf_op jit(solution)/shard_map/psum | solution.py:99
  673.3 1.4 dynamic-slice_multiply_fusion
  (72 shorter events, 1.8 us)
Async XLA Ops:
  7.2 1.0 copy-start
  7.2 4.8 copy-start.10
  7.2 219.7 %all-gather.7.cloned.1.call-start = ((), (), s32[]{:S(2)}) async-start(), calls=%async_computation.1 | async-start | bytes 35651584 | tf_op jit(solution)/shard_map/all_gather | solution.py:11
  12.0 0.6 copy-start.8
  16.2 87.8 %copy-start.4 = (bf16[1,384,4096]{1,2,0:T(8,128)(2,1)}, bf16[1,384,4096]{1,2,0:T(8,128)(2,1)S(1)}, u32[]{:S(2)}) copy-start(bf16[1,384,4096]{1,2,0:T(8,128)(2,1)S(1)} %copy.41) | copy-start | bytes 9437188
  20.0 1.7 copy-start.6
  26.2 399.5 %all-gather.9.cloned.1.call-start = ((), (), s32[]{:S(2)}) async-start(), calls=%async_computation.2 | async-start | bytes 35651584 | tf_op jit(solution)/shard_map/all_gather | solution.py:11
  35.6 5.7 copy-start.12
  41.3 632.0 %all-reduce.4.cloned.1.call-start = ((), (), s32[]{:S(2)}) async-start(), calls=%async_computation | async-start | bytes 1572864 | tf_op jit(solution)/shard_map/psum | solution.py:99
  227.1 198.6 %copy-start.2 = (f32[32,128,128]{2,1,0:T(8,128)}, f32[32,128,128]{2,1,0:T(8,128)S(1)}, u32[]{:S(2)}) copy-start(f32[32,128,128]{2,1,0:T(8,128)S(1)} %get-tuple-element.188) | copy-start | bytes 6291460
  456.5 7.8 %copy-start.3 = (f32[32,128,128]{2,1,0:T(8,128)S(1)}, f32[32,128,128]{2,1,0:T(8,128)}, u32[]{:S(2)}) copy-start(f32[32,128,128]{2,1,0:T(8,128)} %copy-done.2) | copy-start | bytes 6291460
  456.5 7.8 %copy-start.5 = (bf16[1,384,4096]{1,2,0:T(8,128)(2,1)S(1)}, bf16[1,384,4096]{1,2,0:T(8,128)(2,1)}, u32[]{:S(2)}) copy-start(bf16[1,384,4096]{1,2,0:T(8,128)(2,1)} %copy.59) | copy-start | bytes 9437188
  470.9 46.6 %copy-start.9 = (f32[32,384]{1,0:T(8,128)S(1)}, f32[32,384]{1,0:T(8,128)}, u32[]{:S(2)}) copy-start(f32[32,384]{1,0:T(8,128)} %copy-done.8) | copy-start | bytes 147460
  470.9 46.6 %copy-start.11 = (f32[1,32,384]{2,1,0:T(8,128)S(1)}, f32[1,32,384]{2,1,0:T(8,128)}, u32[]{:S(2)}) copy-start(f32[1,32,384]{2,1,0:T(8,128)} %param.19) | copy-start | bytes 147460
  533.1 4.8 copy-start.7
  537.8 136.9 %copy-start.1 = (bf16[6144,32]{0,1:T(8,128)(2,1)S(1)}, bf16[6144,32]{0,1:T(8,128)(2,1)}, u32[]{:S(2)}) copy-start(bf16[6144,32]{0,1:T(8,128)(2,1)} %param.18) | copy-start | bytes 1179652
Sparse Core Ops, SparseCore 0:
  26.3 200.4 all-gather.6
  229.0 196.6 all-gather.8
  522.1 151.1 all-reduce.3
where the time goes:
time: 682 us; the launch traced here: 681 us
  waiting for transfers between devices  442 us (65%)
  matrix products  94.5 us (14%)
  blocking collectives  64 us (9%)
  local copies, waits for them, and re-layouts  33.7 us (5%)
  other arithmetic  31.4 us (5%)
  between operations  14.5 us (2%)
    all_gather x2, waiting for transfers between devices, carried_in(): gathered = jax.tree.map(lambda a: lax.all_gather(a, axis), part)  309 us
    psum x1, waiting for transfers between devices, local(): summed = lax.psum(gate_term, ('dp', 'seq'))  133 us
    unnamed x2, blocking collectives  64 us
    add x15, other arithmetic, combine(): later[0][:, None, None] * earlier[1] + later[1]  29.6 us
    unnamed x37, local copies, waits for them, and re-layouts  28.1 us
    dot_general x1, matrix products, local(): jnp.einsum('hts,thd->shd', mixing, query_rows, preferred_element_type=jnp...  17.3 us
    dot_general x1, matrix products, local(): jnp.einsum('thd,shd->hts', grad_rows, value_rows, preferred_element_type=...  16.3 us
  transfers between devices with their start and end apart: 3, of which 3 were waited for; matrix products, arithmetic and copies ran while one was open for 11% of the time, Pallas kernels for 0%

commit v1 on v0

v1 whole, which is shorter than its diff:
```python
import jax
import jax.numpy as jnp
from jax import lax
from jax.experimental import pallas as pl
from jax.experimental.pallas import tpu as pltpu
from jax.sharding import PartitionSpec as P

F32 = jnp.float32
BF16 = jnp.bfloat16
BLOCK = 384
HEADS = 32
DIM = 128
MODEL = 6144
GROUPS = 16
PER = HEADS // GROUPS
WIDE = PER * DIM
SCALE = 1.0 / DIM
GATE_STEP = 1536
TERM_OWNERS = 2
LIMIT = pltpu.CompilerParams(vmem_limit_bytes=48 * 1024 * 1024)


def dot(a, b, dims):
    return lax.dot_general(a, b, (dims, ((), ())), preferred_element_type=F32)


def as_column(row):
    return jnp.broadcast_to(row, (DIM, BLOCK)).T


def row_sums(rows):
    ones = jnp.ones((8, DIM), BF16)
    high = rows.astype(BF16)
    low = (rows - high.astype(F32)).astype(BF16)
    both = dot(ones, high, ((1,), (1,))) + dot(ones, low, ((1,), (1,)))
    return both[0:1]


def gate_kernel(input_ref, weight_ref, rate_ref, running_ref, slope_ref, logits):
    step = pl.program_id(0)
    part = dot(input_ref[0], weight_ref[...], ((1,), (0,)))

    @pl.when(step == 0)
    def _():
        logits[...] = part

    @pl.when(step > 0)
    def _():
        logits[...] += part

    @pl.when(step == pl.num_programs(0) - 1)
    def _():
        gate_open = jax.nn.sigmoid(logits[...].T)
        log_gate = -2.0 * rate_ref[0] * gate_open
        first = lax.broadcasted_iota(jnp.int32, (BLOCK, BLOCK), 0)
        second = lax.broadcasted_iota(jnp.int32, (BLOCK, BLOCK), 1)
        upper = (first <= second).astype(F32)
        running_ref[...] = jnp.dot(
            log_gate, upper, precision=lax.Precision.HIGHEST, preferred_element_type=F32
        )
        slope_ref[...] = log_gate * (1.0 - gate_open)


def state_kernel(query_ref, key_ref, value_ref, grad_ref, running_ref, out_ref):
    fades = []
    for j in range(PER):
        cols = slice(j * DIM, (j + 1) * DIM)
        row = running_ref[0, j : j + 1, :]
        column = as_column(row)
        total = row[:, BLOCK - 1 : BLOCK]
        key_faded = (key_ref[0, :, cols].astype(F32) * jnp.exp(total - column)).astype(BF16)
        query_faded = (query_ref[0, :, cols].astype(F32) * jnp.exp(column)).astype(BF16)
        base = 2 * DIM * j
        out_ref[0, base : base + DIM, :] = dot(key_faded, value_ref[0, :, cols], ((0,), (0,)))
        out_ref[0, base + DIM : base + 2 * DIM, :] = dot(
            query_faded, grad_ref[0, :, cols], ((0,), (0,))
        )
        fades.append(jnp.broadcast_to(jnp.exp(total), (8, DIM)))
    place = lax.broadcasted_iota(jnp.int32, (8, DIM), 0)
    out_ref[0, 2 * DIM * PER :, :] = jnp.where(place == 0, fades[0], fades[1])


def scan_kernel(states_ref, fades_ref, out_ref):
    head = pl.program_id(0)
    out_ref[0, :DIM, :] = jnp.zeros((DIM, DIM), F32)
    out_ref[GROUPS - 1, DIM:, :] = jnp.zeros((DIM, DIM), F32)
    for n in range(GROUPS - 1):
        fade = fades_ref[n, pl.ds(head, 1), :]
        out_ref[n + 1, :DIM, :] = states_ref[n, :DIM, :] + fade * out_ref[n, :DIM, :]
        m = GROUPS - 1 - n
        fade = fades_ref[m, pl.ds(head, 1), :]
        out_ref[m - 1, DIM:, :] = states_ref[m, DIM:, :] + fade * out_ref[m, DIM:, :]


def local_kernel(
    query_ref, key_ref, value_ref, grad_ref, running_ref, ql_ref, kl_ref, vl_ref, push_ref
):
    first = lax.broadcasted_iota(jnp.int32, (BLOCK, BLOCK), 0)
    second = lax.broadcasted_iota(jnp.int32, (BLOCK, BLOCK), 1)
    causal = first >= second
    for j in range(PER):
        cols = slice(j * DIM, (j + 1) * DIM)
        row = running_ref[0, j : j + 1, :]
        column = jnp.broadcast_to(row, (DIM, BLOCK)).T
        column = jnp.concatenate([column] * (BLOCK // DIM), axis=1)
        decay = jnp.exp(jnp.where(causal, column - row, -1e30)) * SCALE
        query, key = query_ref[0, :, cols], key_ref[0, :, cols]
        value, grad = value_ref[0, :, cols], grad_ref[0, :, cols]
        weighted = (dot(query, key, ((1,), (1,))) * decay).astype(BF16)
        mixing = (dot(grad, value, ((1,), (1,))) * decay).astype(BF16)
        query_local = dot(mixing, key, ((1,), (0,)))
        key_local = dot(mixing, query, ((0,), (0,)))
        ql_ref[:, cols] = query_local
        kl_ref[:, cols] = key_local
        vl_ref[:, cols] = dot(weighted, grad, ((0,), (0,)))
        push_ref[0, j : j + 1, :] = row_sums(
            query.astype(F32) * query_local - key.astype(F32) * key_local
        )


def push_kernel(
    query_ref, key_ref, value_ref, grad_ref, running_ref, carried_ref, local_ref, push_ref
):
    last = lax.broadcasted_iota(jnp.int32, (1, BLOCK), 1) == BLOCK - 1
    for j in range(PER):
        cols = slice(j * DIM, (j + 1) * DIM)
        base = 2 * DIM * j
        row = running_ref[0, j : j + 1, :]
        column = as_column(row)
        total = row[:, BLOCK - 1 : BLOCK]
        prior = carried_ref[0, base : base + DIM, :]
        later = carried_ref[0, base + DIM : base + 2 * DIM, :]
        query_state = dot(grad_ref[0, :, cols], prior.astype(BF16), ((1,), (1,)))
        key_state = dot(value_ref[0, :, cols], later.astype(BF16), ((1,), (1,)))
        from_query = query_ref[0, :, cols].astype(F32) * query_state * (jnp.exp(column) * SCALE)
        from_key = (
            key_ref[0, :, cols].astype(F32) * key_state * (jnp.exp(total - column) * SCALE)
        )
        crossing = jnp.sum(from_key, axis=0, keepdims=True) + (
            jnp.exp(total) * SCALE
        ) * jnp.sum(prior * later, axis=0, keepdims=True)
        tail = jnp.sum(crossing, axis=1, keepdims=True)
        push = row_sums(from_query - from_key) + local_ref[0, j : j + 1, :]
        push_ref[0, j : j + 1, :] = push + jnp.where(last, tail, 0.0)


def term_kernel(push_ref, slope_ref, input_ref, out_ref, logit_grad):
    @pl.when(pl.program_id(0) == 0)
    def _():
        first = lax.broadcasted_iota(jnp.int32, (BLOCK, BLOCK), 0)
        second = lax.broadcasted_iota(jnp.int32, (BLOCK, BLOCK), 1)
        lower = (first >= second).astype(F32)
        gate_grad = jnp.dot(
            push_ref[...], lower, precision=lax.Precision.HIGHEST, preferred_element_type=F32
        )
        logit_grad[...] = (gate_grad * slope_ref[...]).astype(BF16)

    for i in range(TERM_OWNERS):
        cols = slice(i * BLOCK, (i + 1) * BLOCK)
        out_ref[i] = dot(logit_grad[...], input_ref[0, :, cols], ((1,), (0,)))


def full_kernel(
    key_ref, value_ref, grad_ref, running_ref, carried_ref, ql_ref, kl_ref, vl_ref,
    query_out, key_out, value_out,
):
    for j in range(PER):
        cols = slice(j * DIM, (j + 1) * DIM)
        base = 2 * DIM * j
        row = running_ref[0, j : j + 1, :]
        column = as_column(row)
        total = row[:, BLOCK - 1 : BLOCK]
        from_start = jnp.exp(column) * SCALE
        to_end = jnp.exp(total - column) * SCALE
        prior = carried_ref[0, base : base + DIM, :].astype(BF16)
        later = carried_ref[0, base + DIM : base + 2 * DIM, :].astype(BF16)
        query_out[0, :, cols] = (
            ql_ref[:, cols] + from_start * dot(grad_ref[0, :, cols], prior, ((1,), (1,)))
        ).astype(BF16)
        key_out[0, :, cols] = (
            kl_ref[:, cols] + to_end * dot(value_ref[0, :, cols], later, ((1,), (1,)))
        ).astype(BF16)
        value_out[0, :, cols] = (
            vl_ref[:, cols] + to_end * dot(key_ref[0, :, cols], later, ((1,), (0,)))
        ).astype(BF16)


def heads_block():
    return pl.BlockSpec((1, BLOCK, WIDE), lambda i: (0, 0, i))


def rows_block():
    return pl.BlockSpec((1, PER, BLOCK), lambda i: (i, 0, 0))


def flat_block():
    return pl.BlockSpec((BLOCK, WIDE), lambda i: (0, i))


def local(query_heads, key_heads, value_heads, output_grad, layer_input, gate_weight, decay_rate):
    shape = jax.ShapeDtypeStruct
    rows = 2 * DIM * PER
    whole = pl.BlockSpec((HEADS, BLOCK), lambda i: (0, 0))
    running, slope = pl.pallas_call(
        gate_kernel,
        grid=(MODEL // GATE_STEP,),
        in_specs=[
            pl.BlockSpec((1, BLOCK, GATE_STEP), lambda i: (0, 0, i)),
            pl.BlockSpec((GATE_STEP, HEADS), lambda i: (i, 0)),
            pl.BlockSpec((1, HEADS, BLOCK), lambda i: (0, 0, 0)),
        ],
        out_specs=[whole, whole],
        out_shape=[shape((HEADS, BLOCK), F32)] * 2,
        scratch_shapes=[pltpu.VMEM((BLOCK, HEADS), F32)],
        compiler_params=LIMIT,
        name="gates",
    )(layer_input, gate_weight, decay_rate)
    running = running.reshape(GROUPS, PER, BLOCK)
    carried_block = pl.BlockSpec((1, rows, DIM), lambda i: (i, 0, 0))
    states = pl.pallas_call(
        state_kernel,
        grid=(GROUPS,),
        in_specs=[heads_block()] * 4 + [rows_block()],
        out_specs=pl.BlockSpec((1, rows + 8, DIM), lambda i: (i, 0, 0)),
        out_shape=shape((GROUPS, rows + 8, DIM), F32),
        compiler_params=LIMIT,
        name="states",
    )(query_heads, key_heads, value_heads, output_grad, running)
    states = lax.all_to_all(states, "seq", 0, 0, tiled=True)
    query_local, key_local, value_local, local_push = pl.pallas_call(
        local_kernel,
        grid=(GROUPS,),
        in_specs=[heads_block()] * 4 + [rows_block()],
        out_specs=[flat_block()] * 3 + [rows_block()],
        out_shape=[shape((BLOCK, HEADS * DIM), F32)] * 3 + [shape((GROUPS, PER, BLOCK), F32)],
        compiler_params=LIMIT,
        name="locals",
    )(query_heads, key_heads, value_heads, output_grad, running)
    carried = pl.pallas_call(
        scan_kernel,
        grid=(PER,),
        in_specs=[
            pl.BlockSpec((GROUPS, 2 * DIM, DIM), lambda i: (0, i, 0)),
            pl.BlockSpec((GROUPS, 8, DIM), lambda i: (0, rows // 8, 0)),
        ],
        out_specs=pl.BlockSpec((GROUPS, 2 * DIM, DIM), lambda i: (0, i, 0)),
        out_shape=shape((GROUPS, rows, DIM), F32),
        compiler_params=LIMIT,
        name="scan",
    )(states, states)
    carried = lax.all_to_all(carried, "seq", 0, 0, tiled=True)
    push = pl.pallas_call(
        push_kernel,
        grid=(GROUPS,),
        in_specs=[heads_block()] * 4 + [rows_block(), carried_block, rows_block()],
        out_specs=rows_block(),
        out_shape=shape((GROUPS, PER, BLOCK), F32),
        compiler_params=LIMIT,
        name="push",
    )(query_heads, key_heads, value_heads, output_grad, running, carried, local_push)
    terms = pl.pallas_call(
        term_kernel,
        grid=(GROUPS // TERM_OWNERS,),
        in_specs=[
            whole,
            whole,
            pl.BlockSpec((1, BLOCK, TERM_OWNERS * BLOCK), lambda i: (0, 0, i)),
        ],
        out_specs=pl.BlockSpec((TERM_OWNERS, HEADS, BLOCK), lambda i: (i, 0, 0)),
        out_shape=shape((GROUPS, HEADS, BLOCK), F32),
        scratch_shapes=[pltpu.VMEM((HEADS, BLOCK), BF16)],
        compiler_params=LIMIT,
        name="terms",
    )(push.reshape(HEADS, BLOCK), slope, layer_input)
    terms = jnp.sum(lax.all_to_all(terms, "seq", 0, 0, tiled=True), axis=0)
    query_grad, key_grad, value_grad = pl.pallas_call(
        full_kernel,
        grid=(GROUPS,),
        in_specs=[heads_block()] * 3 + [rows_block(), carried_block] + [flat_block()] * 3,
        out_specs=[heads_block()] * 3,
        out_shape=[shape((1, BLOCK, HEADS * DIM), BF16)] * 3,
        compiler_params=LIMIT,
        name="full",
    )(
        key_heads, value_heads, output_grad, running, carried,
        query_local, key_local, value_local,
    )
    token_count = BLOCK * lax.axis_size("seq") * lax.axis_size("dp")
    weight_grad = jnp.sum(lax.all_gather(terms, "dp"), axis=0) / token_count
    return query_grad, key_grad, value_grad, weight_grad


def solution(mesh):
    heads = P("dp", "seq", None)
    return jax.shard_map(
        local,
        mesh=mesh,
        in_specs=(heads,) * 5 + (P(), P("dp", None, "seq")),
        out_specs=(heads,) * 3 + (P(None, "seq"),),
        check_vma=False,
    )
```

time: 682 us -> 218 us (0.32)
  waiting for transfers between devices: 442 us -> 34.9 us
  matrix products: 94.5 us -> 0 us
  Pallas kernels: 0 us -> 84.7 us
  other arithmetic: 31.4 us -> 1.83 us
  local copies, waits for them, and re-layouts: 33.7 us -> 10.2 us
  between operations: 14.5 us -> 0.76 us
  blocking collectives: 64 us -> 75.1 us
  starting transfers between devices: 0.12 us -> 8.83 us
    all_gather x2 -> x0, waiting for transfers between devices: 309 us -> none  [carried_in(): gathered = jax.tree.map(lambda a: lax.all_gather(a, axis), part)]
    psum x1 -> x0, waiting for transfers between devices: 133 us -> none  [local(): summed = lax.psum(gate_term, ('dp', 'seq'))]
    dot_general x13 -> x0, matrix products: 94.5 us -> none  [the longest x1 17.3 us: local(): jnp.einsum('hts,thd->shd', mixing, query_rows, preferred_element_type=jnp...]
    pallas_call x0 -> x7, Pallas kernels: none -> 84.7 us  [the longest x1 24.6 us: local(): pl.pallas_call(local_kernel, grid=(GROUPS,), in_specs=[heads_block()] * 4...]
    unnamed x2 -> x0, blocking collectives: 64 us -> none
    all_to_all x0 -> x1, blocking collectives: none -> 58.3 us  [local(): states = lax.all_to_all(states, 'seq', 0, 0, tiled=True)]
    all_to_all x0 -> x2, waiting for transfers between devices: none -> 34.9 us  [the longest x1 34.9 us: local(): carried = lax.all_to_all(carried, 'seq', 0, 0, tiled=True)]
    add x30 -> x0, other arithmetic: 29.9 us -> none  [the longest x15 29.6 us: combine(): later[0][:, None, None] * earlier[1] + later[1]]
  transfers between devices with their start and end apart: 3 -> 2, of which waited for: 3 -> 1; matrix products, arithmetic and copies ran while one was open for 11% -> 0% of each run, Pallas kernels for 0% -> 20%
where the time goes in v1:
time: 218 us; the launch traced here: 216 us
  Pallas kernels  84.7 us (39%)
  blocking collectives  75.1 us (34%)
  waiting for transfers between devices  34.9 us (16%)
  local copies, waits for them, and re-layouts  10.2 us (5%)
  starting transfers between devices  8.83 us (4%)
    all_to_all x1, blocking collectives, local(): states = lax.all_to_all(states, 'seq', 0, 0, tiled=True)  58.3 us
    all_to_all x1, waiting for transfers between devices, local(): carried = lax.all_to_all(carried, 'seq', 0, 0, tiled=True)  34.9 us
    pallas_call x1, Pallas kernels, local(): pl.pallas_call(local_kernel, grid=(GROUPS,), in_specs=[heads_block()] * 4...  24.6 us
    pallas_call x1, Pallas kernels, local(): pl.pallas_call(full_kernel, grid=(GROUPS,), in_specs=[heads_block()] * 3...  19 us
    all_gather x1, blocking collectives, local(): weight_grad = jnp.sum(lax.all_gather(terms, 'dp'), axis=0) / token_count  16.8 us
    pallas_call x1, Pallas kernels, local(): pl.pallas_call(push_kernel, grid=(GROUPS,), in_specs=[heads_block()] * 4...  16.8 us
    pallas_call x1, Pallas kernels, local(): pl.pallas_call(state_kernel, grid=(GROUPS,), in_specs=[heads_block()] * 4...  14.9 us
    unnamed x15, local copies, waits for them, and re-layouts  10.1 us
  transfers between devices with their start and end apart: 2, of which 1 were waited for; matrix products, arithmetic and copies ran while one was open for 0% of the time, Pallas kernels for 20%

profile of v1, /device:TPU:1, one launch (start us, length us, event | category | flops | bytes accessed | tf_op | source)
XLA Modules:
  0.0 216.4 jit_solution(10700252082732507742)
XLA Ops:
  0.6 0.0 copy-start.1
  0.6 2.5 %copy.12.weight_ref = bf16[6144,32]{1,0:T(8,128)(2,1)} copy(bf16[6144,32]{0,1:T(8,128)(2,1)} %param.12) | data formatting | bytes 786432 | tf_op args[5]
  3.2 0.0 copy-start.4
  3.2 1.4 copy-done.4
  4.6 0.0 copy-start.6
  4.6 0.8 copy-done.6
  5.4 4.5 %gates.1 = (f32[32,384]{1,0:T(8,128)S(1)}, f32[32,384]{1,0:T(8,128)S(1)}) custom-call(bf16[1,384,6144]{2,1,0:T(8,128)(2,1)} %input_ref.3, bf16[6144,32]{1,0:T(8,128)(2,1)S(1)} %copy-done.4, f32[1,32,384]{2,1,0:T(8,128)S(1)} %copy-done.6), custom_call_target="tpu_custom_call" | custom-call | tf_op jit(solution)/shard_map/gates/pallas_call | solution.py:204
  10.0 0.0 copy-done.1
  10.0 14.9 %states.1 = f32[16,520,128]{2,1,0:T(8,128)} custom-call(bf16[1,384,4096]{2,1,0:T(8,128)(2,1)S(1)} %copy-done.1, bf16[1,384,4096]{2,1,0:T(8,128)(2,1)} %key_ref.7, bf16[1,384,4096]{2,1,0:T(8,128)(2,1)} %value_ref.7, bf16[1,384,4096]{2,1,0:T(8,128)(2,1)} %grad_ref.7, f32[16,2,384]{2,1,0:T(2,128)S(1)} %reshape.14.running_ref), custom_call_target="tpu_custom_call" | custom-call | tf_op jit(solution)/shard_map/states/pallas_call | solution.py:220
  24.9 58.3 %all_to_all.15.states_ref.fades_ref = f32[16,520,128]{2,1,0:T(8,128)} all-to-all(f32[16,520,128]{2,1,0:T(8,128)} %states.1), channel_id=1, replica_groups=mesh['dp'=8,'seq'=16] {'seq'}, dimensions={0} | all-to-all | bytes 8519680 | tf_op jit(solution)/shard_map/all_to_all | solution.py:229
  83.2 2.6 %scan.1 = f32[16,512,128]{2,1,0:T(8,128)S(1)} custom-call(f32[16,520,128]{2,1,0:T(8,128)} %all_to_all.15.states_ref.fades_ref, f32[16,520,128]{2,1,0:T(8,128)} %all_to_all.15.states_ref.fades_ref), custom_call_target="tpu_custom_call" | custom-call | tf_op jit(solution)/shard_map/scan/pallas_call | solution.py:239
  85.7 0.0 copy-start.3
  85.7 2.0 copy-done.3
  87.8 4.5 %all-to-all-start.1 = ((f32[16,512,128]{2,1,0:T(8,128)}), f32[16,512,128]{2,1,0:T(8,128)}, u32[]{:S(2)}, u32[]{:S(2)}) async-start(f32[16,512,128]{2,1,0:T(8,128)} %copy-done.3), calls=%async_computation.1 | async-start | bytes 8388608 | tf_op jit(solution)/shard_map/all_to_all | solution.py:251
  92.3 24.6 %locals.1 = (f32[384,4096]{1,0:T(8,128)}, f32[384,4096]{1,0:T(8,128)}, f32[384,4096]{1,0:T(8,128)}, f32[16,2,384]{2,1,0:T(2,128)S(1)}) custom-call(bf16[1,384,4096]{2,1,0:T(8,128)(2,1)S(1)} %copy-done.1, bf16[1,384,4096]{2,1,0:T(8,128)(2,1)} %key_ref.7, bf16[1,384,4096]{2,1,0:T(8,128)(2,1)} %value_ref.7, bf16[1,384,4096]{2,1,0:T(8,128)(2,1)} %grad_ref.7, ...), custom_call_target="tpu_custom_call" | custom-call | tf_op jit(solution)/shard_map/locals/pallas_call | solution.py:230
  116.9 34.9 %all-to-all-done.1.carried_ref = f32[16,512,128]{2,1,0:T(8,128)} async-done(((f32[16,512,128]{2,1,0:T(8,128)}), f32[16,512,128]{2,1,0:T(8,128)}, u32[]{:S(2)}, u32[]{:S(2)}) %all-to-all-start.1) | async-done | bytes 4194336 | tf_op jit(solution)/shard_map/all_to_all | solution.py:251
  151.8 16.8 %push.1 = f32[16,2,384]{2,1,0:T(2,128)S(1)} custom-call(bf16[1,384,4096]{2,1,0:T(8,128)(2,1)S(1)} %copy-done.1, bf16[1,384,4096]{2,1,0:T(8,128)(2,1)} %key_ref.7, bf16[1,384,4096]{2,1,0:T(8,128)(2,1)} %value_ref.7, bf16[1,384,4096]{2,1,0:T(8,128)(2,1)} %grad_ref.7, f32[16,2,384]{2,1,0:T(2,128)S(1)} %reshape.14.running_ref, ...), custom_call_target="tpu_custom_call" | custom-call | tf_op jit(solution)/shard_map/push/pallas_call | solution.py:252
  168.6 0.0 copy-start
  168.6 0.0 copy-start.2
  168.6 2.5 %copy-done.2 = bf16[1,384,6144]{2,1,0:T(8,128)(2,1)S(1)} copy-done((bf16[1,384,6144]{2,1,0:T(8,128)(2,1)S(1)}, bf16[1,384,6144]{2,1,0:T(8,128)(2,1)}, u32[]{:S(2)}) %copy-start.2) | copy-done | bytes 4718616
  171.1 2.4 %terms.1 = f32[16,32,384]{2,1,0:T(8,128)S(1)} custom-call(f32[32,384]{1,0:T(8,128)S(1)} %reshape.15.push_ref, f32[32,384]{1,0:T(8,128)S(1)} %get-tuple-element.21.slope_ref, bf16[1,384,6144]{2,1,0:T(8,128)(2,1)S(1)} %copy-done.2), custom_call_target="tpu_custom_call" | custom-call | tf_op jit(solution)/shard_map/terms/pallas_call | solution.py:261
  173.5 0.0 copy-start.5
  173.5 0.9 copy-done.5
  174.4 4.3 %all-to-all-start.2 = ((f32[16,32,384]{2,1,0:T(8,128)}), f32[16,32,384]{2,1,0:T(8,128)}, u32[]{:S(2)}, u32[]{:S(2)}) async-start(f32[16,32,384]{2,1,0:T(8,128)} %copy-done.5), calls=%async_computation.2 | async-start | bytes 1572864 | tf_op jit(solution)/shard_map/all_to_all | solution.py:275
  178.6 0.0 copy-done
  178.7 19.0 %full.1 = (bf16[1,384,4096]{2,1,0:T(8,128)(2,1)}, bf16[1,384,4096]{2,1,0:T(8,128)(2,1)}, bf16[1,384,4096]{2,1,0:T(8,128)(2,1)}) custom-call(bf16[1,384,4096]{2,1,0:T(8,128)(2,1)S(1)} %copy-done, bf16[1,384,4096]{2,1,0:T(8,128)(2,1)} %value_ref.7, bf16[1,384,4096]{2,1,0:T(8,128)(2,1)} %grad_ref.7, f32[16,2,384]{2,1,0:T(2,128)S(1)} %reshape.14.running_ref, ...), custom_call_target="tpu_custom_call" | custom-call | tf_op jit(solution)/shard_map/full/pallas_call | solution.py:276
  197.7 0.0 all-to-all-done.2
  197.7 1.2 reduce_sum.18
  198.9 16.8 %all-gather = f32[256,384]{1,0:T(8,128)S(1)} all-gather(f32[32,384]{1,0:T(8,128)S(1)} %reduce_sum.18), channel_id=2, replica_groups=mesh['dp'=8,'seq'=16] {'dp'}, dimensions={0}, use_global_device_ids=true | all-gather | bytes 442368 | tf_op jit(solution)/shard_map/all_gather | solution.py:289
  215.7 0.6 broadcast_multiply_fusion
  (3 shorter events, 0.1 us)
Async XLA Ops:
  0.6 9.3 %copy-start.1 = (bf16[1,384,4096]{2,1,0:T(8,128)(2,1)S(1)}, bf16[1,384,4096]{2,1,0:T(8,128)(2,1)}, u32[]{:S(2)}) copy-start(bf16[1,384,4096]{2,1,0:T(8,128)(2,1)} %query_ref.5) | copy-start | bytes 9437188
  3.2 1.4 copy-start.4
  4.6 0.8 copy-start.6
  85.7 2.0 copy-start.3
  87.8 64.0 %all-to-all-start.1 = ((f32[16,512,128]{2,1,0:T(8,128)}), f32[16,512,128]{2,1,0:T(8,128)}, u32[]{:S(2)}, u32[]{:S(2)}) async-start(f32[16,512,128]{2,1,0:T(8,128)} %copy-done.3), calls=%async_computation.1 | async-start | bytes 8388608 | tf_op jit(solution)/shard_map/all_to_all | solution.py:251
  168.6 10.1 %copy-start = (bf16[1,384,4096]{2,1,0:T(8,128)(2,1)S(1)}, bf16[1,384,4096]{2,1,0:T(8,128)(2,1)}, u32[]{:S(2)}) copy-start(bf16[1,384,4096]{2,1,0:T(8,128)(2,1)} %key_ref.7) | copy-start | bytes 9437188
  168.6 2.5 %copy-start.2 = (bf16[1,384,6144]{2,1,0:T(8,128)(2,1)S(1)}, bf16[1,384,6144]{2,1,0:T(8,128)(2,1)}, u32[]{:S(2)}) copy-start(bf16[1,384,6144]{2,1,0:T(8,128)(2,1)} %input_ref.3) | copy-start | bytes 14155780
  173.5 0.9 copy-start.5
  174.4 23.3 %all-to-all-start.2 = ((f32[16,32,384]{2,1,0:T(8,128)}), f32[16,32,384]{2,1,0:T(8,128)}, u32[]{:S(2)}, u32[]{:S(2)}) async-start(f32[16,32,384]{2,1,0:T(8,128)} %copy-done.5), calls=%async_computation.2 | async-start | bytes 1572864 | tf_op jit(solution)/shard_map/all_to_all | solution.py:275

commit v2 on v0

v2 whole, which is shorter than its diff:
```python
import jax
import jax.numpy as jnp
from jax import lax
from jax.experimental import pallas as pl
from jax.experimental.pallas import tpu as pltpu
from jax.sharding import PartitionSpec as P

F32 = jnp.float32
BF16 = jnp.bfloat16
BLOCK = 384
HEADS = 32
DIM = 128
MODEL = 6144
GROUPS = 16
PER = HEADS // GROUPS
ROWS = 2 * DIM + 8
SCALE = 1.0 / DIM
GATE_STEP = 3072
GATE_STEPS = MODEL // GATE_STEP
STATE_HEADS = 8
LOCAL_HEADS = 2
TERM_HEADS = 8
TERM_STEPS = HEADS // TERM_HEADS
FULL_HEADS = 8
TERM_OWNERS = 8
SCAN_MIB, TERM_MIB, FULL_MIB = 60, 60, 60


def limit(mib):
    return pltpu.CompilerParams(vmem_limit_bytes=mib * 1024 * 1024)


def dot(a, b, dims):
    return lax.dot_general(a, b, (dims, ((), ())), preferred_element_type=F32)


def rounded_sum(rounded, other):
    return jnp.sum(rounded.astype(BF16).astype(F32) * other, axis=0, keepdims=True) * SCALE


def as_column(row):
    return jnp.broadcast_to(row, (DIM, BLOCK)).T


def row_sums(rows):
    ones = jnp.ones((8, DIM), BF16)
    high = rows.astype(BF16)
    low = (rows - high.astype(F32)).astype(BF16)
    both = dot(ones, high, ((1,), (1,))) + dot(ones, low, ((1,), (1,)))
    return both[0:1]


def state_kernel(
    input_ref, weight_ref, rate_ref, query_ref, key_ref, value_ref, grad_ref,
    running_ref, slope_ref, decay_ref, out_ref, logits,
):
    step = pl.program_id(0)

    @pl.when(step == 0)
    def _():
        logits[...] = dot(weight_ref[...], input_ref[0], ((1,), (1,)))

    @pl.when((step > 0) & (step < GATE_STEPS))
    def _():
        logits[...] += dot(weight_ref[...], input_ref[0], ((1,), (1,)))

    @pl.when(step == GATE_STEPS - 1)
    def _():
        gate_open = jax.nn.sigmoid(logits[...])
        log_gate = -2.0 * rate_ref[0] * gate_open
        first = lax.broadcasted_iota(jnp.int32, (BLOCK, BLOCK), 0)
        second = lax.broadcasted_iota(jnp.int32, (BLOCK, BLOCK), 1)
        upper = (first <= second).astype(F32)
        running = jnp.dot(
            log_gate, upper, precision=lax.Precision.HIGHEST, preferred_element_type=F32
        )
        running_ref[...] = running
        slope_ref[...] = log_gate * (1.0 - gate_open)
        decay_ref[:HEADS, :] = jnp.exp(running)
        decay_ref[HEADS:, :] = jnp.exp(running[:, BLOCK - 1 : BLOCK] - running)

    @pl.when(step >= GATE_STEPS)
    def _():
        for j in range(STATE_HEADS):
            cols = slice(j * DIM, (j + 1) * DIM)
            head = (step - GATE_STEPS) * STATE_HEADS + j
            from_start = decay_ref[pl.ds(head, 1), :]
            to_end = decay_ref[pl.ds(HEADS + head, 1), :]
            key_faded = (key_ref[0, :, cols].T.astype(F32) * to_end).astype(BF16)
            query_faded = (query_ref[0, :, cols].T.astype(F32) * from_start).astype(BF16)
            out_ref[j, :DIM, :] = dot(key_faded, value_ref[0, :, cols], ((1,), (0,)))
            out_ref[j, DIM : 2 * DIM, :] = dot(query_faded, grad_ref[0, :, cols], ((1,), (0,)))
            out_ref[j, 2 * DIM :, :] = jnp.broadcast_to(
                from_start[:, BLOCK - 1 : BLOCK], (8, DIM)
            )


def scan_kernel(states_ref, out_ref):
    early, late, own = slice(0, DIM), slice(DIM, 2 * DIM), slice(2 * DIM, 2 * DIM + 1)
    prior = jnp.zeros((DIM, DIM), F32)
    pushes = []
    for n in range(GROUPS):
        out_ref[n, :DIM, :] = prior
        pushes.append(rounded_sum(prior, states_ref[n, late, :]))
        prior = states_ref[n, early, :] + states_ref[n, own, :] * prior
    later = jnp.zeros((DIM, DIM), F32)
    tail = jnp.zeros((1, DIM), F32)
    for n in reversed(range(GROUPS)):
        out_ref[n, DIM : 2 * DIM, :] = later
        out_ref[n, 2 * DIM :, :] = jnp.broadcast_to(tail, (8, DIM))
        tail = tail + pushes[n] - rounded_sum(later, states_ref[n, early, :])
        later = states_ref[n, late, :] + states_ref[n, own, :] * later


def local_kernel(
    query_ref, key_ref, value_ref, grad_ref, running_ref,
    ql_ref, kl_ref, vl_ref, qt_ref, kt_ref, push_ref,
):
    first = lax.broadcasted_iota(jnp.int32, (BLOCK, BLOCK), 0)
    second = lax.broadcasted_iota(jnp.int32, (BLOCK, BLOCK), 1)
    causal = first >= second
    for j in range(LOCAL_HEADS):
        cols = slice(j * DIM, (j + 1) * DIM)
        head = pl.ds(pl.program_id(0) * LOCAL_HEADS + j, 1)
        row = running_ref[head, :]
        column = jnp.concatenate([as_column(row)] * (BLOCK // DIM), axis=1)
        decay = jnp.exp(jnp.where(causal, column - row, -1e30)) * SCALE
        query, key = query_ref[0, :, cols], key_ref[0, :, cols]
        value, grad = value_ref[0, :, cols], grad_ref[0, :, cols]
        weighted = (dot(query, key, ((1,), (1,))) * decay).astype(BF16)
        mixing = (dot(grad, value, ((1,), (1,))) * decay).astype(BF16)
        query_local = dot(mixing, key, ((1,), (0,)))
        key_local = dot(mixing, query, ((0,), (0,)))
        qt_ref[cols, :] = query.T
        kt_ref[cols, :] = key.T
        ql_ref[:, cols] = query_local
        kl_ref[:, cols] = key_local
        vl_ref[:, cols] = dot(weighted, grad, ((0,), (0,)))
        push_ref[head, :] = row_sums(
            query.astype(F32) * query_local - key.astype(F32) * key_local
        )


def term_kernel(
    query_ref, key_ref, value_ref, grad_ref, decay_ref, carried_ref, local_ref, slope_ref,
    input_ref, out_ref, push,
):
    step = pl.program_id(0)

    @pl.when(step < TERM_STEPS)
    def _():
        last = lax.broadcasted_iota(jnp.int32, (1, BLOCK), 1) == BLOCK - 1
        for j in range(TERM_HEADS):
            head = step * TERM_HEADS + j
            cols = slice(j * DIM, (j + 1) * DIM)
            prior = carried_ref[j, :DIM, :].astype(BF16)
            later = carried_ref[j, DIM : 2 * DIM, :].astype(BF16)
            query_state = dot(prior, grad_ref[0, :, cols], ((1,), (1,)))
            key_state = dot(later, value_ref[0, :, cols], ((1,), (1,)))
            from_query = jnp.sum(
                query_ref[cols, :].astype(F32) * query_state, axis=0, keepdims=True
            ) * (decay_ref[pl.ds(head, 1), :] * SCALE)
            from_key = jnp.sum(
                key_ref[cols, :].astype(F32) * key_state, axis=0, keepdims=True
            ) * (decay_ref[pl.ds(HEADS + head, 1), :] * SCALE)
            tail = jnp.sum(carried_ref[j, 2 * DIM : 2 * DIM + 1, :], axis=1, keepdims=True)
            push[pl.ds(head, 1), :] = (
                from_query - from_key + local_ref[pl.ds(head, 1), :] + jnp.where(last, tail, 0.0)
            )

    @pl.when(step == TERM_STEPS - 1)
    def _():
        first = lax.broadcasted_iota(jnp.int32, (BLOCK, BLOCK), 0)
        second = lax.broadcasted_iota(jnp.int32, (BLOCK, BLOCK), 1)
        lower = (first >= second).astype(F32)
        gate_grad = jnp.dot(
            push[...], lower, precision=lax.Precision.HIGHEST, preferred_element_type=F32
        )
        push[...] = gate_grad * slope_ref[...]

    @pl.when(step >= TERM_STEPS)
    def _():
        logit_grad = push[...].astype(BF16)
        for i in range(TERM_OWNERS):
            cols = slice(i * BLOCK, (i + 1) * BLOCK)
            out_ref[i] = dot(logit_grad, input_ref[0, :, cols], ((1,), (0,)))


def query_kernel(
    value_ref, grad_ref, decay_ref, carried_ref, ql_ref, kl_ref, query_out, key_out
):
    for j in range(FULL_HEADS):
        cols = slice(j * DIM, (j + 1) * DIM)
        head = pl.program_id(0) * FULL_HEADS + j
        from_start = as_column(decay_ref[pl.ds(head, 1), :] * SCALE)
        to_end = as_column(decay_ref[pl.ds(HEADS + head, 1), :] * SCALE)
        prior = carried_ref[j, :DIM, :].astype(BF16)
        later = carried_ref[j, DIM : 2 * DIM, :].astype(BF16)
        query_out[0, :, cols] = (
            ql_ref[:, cols] + from_start * dot(grad_ref[0, :, cols], prior, ((1,), (1,)))
        ).astype(BF16)
        key_out[0, :, cols] = (
            kl_ref[:, cols] + to_end * dot(value_ref[0, :, cols], later, ((1,), (1,)))
        ).astype(BF16)


def value_kernel(key_ref, decay_ref, carried_ref, vl_ref, value_out):
    for j in range(FULL_HEADS):
        cols = slice(j * DIM, (j + 1) * DIM)
        head = pl.program_id(0) * FULL_HEADS + j
        to_end = as_column(decay_ref[pl.ds(HEADS + head, 1), :] * SCALE)
        later = carried_ref[j, DIM : 2 * DIM, :].astype(BF16)
        value_out[0, :, cols] = (
            vl_ref[:, cols] + to_end * dot(key_ref[0, :, cols], later, ((1,), (0,)))
        ).astype(BF16)


def same(i):
    return i


def heads_block(heads, group=same):
    return pl.BlockSpec((1, BLOCK, heads * DIM), lambda i: (0, 0, group(i)))


def carried_block(heads, group=same):
    return pl.BlockSpec((heads, ROWS, DIM), lambda i: (group(i), 0, 0))


def flat_block(heads, group=same):
    return pl.BlockSpec((BLOCK, heads * DIM), lambda i: (0, group(i)))


def turned_block(heads, group=same):
    return pl.BlockSpec((heads * DIM, BLOCK), lambda i: (group(i), 0))


def whole_block(*dims):
    return pl.BlockSpec(dims, lambda i: (0,) * len(dims))


shape = jax.ShapeDtypeStruct
ROW_TABLE = (HEADS, BLOCK)
DECAY_TABLE = (2 * HEADS, BLOCK)
TRAVELLING = (HEADS, ROWS, DIM)
OUT = (1, BLOCK, HEADS * DIM)


def states_of(layer_input, gate_weight, decay_rate, *heads):
    def feature(i):
        return jnp.minimum(i, GATE_STEPS - 1)

    def behind(i):
        return jnp.maximum(i - GATE_STEPS, 0)

    return pl.pallas_call(
        state_kernel,
        grid=(GATE_STEPS + HEADS // STATE_HEADS,),
        in_specs=[
            pl.BlockSpec((1, BLOCK, GATE_STEP), lambda i: (0, 0, feature(i))),
            pl.BlockSpec((HEADS, GATE_STEP), lambda i: (0, feature(i))),
            whole_block(1, HEADS, BLOCK),
        ]
        + [heads_block(STATE_HEADS, behind)] * 4,
        out_specs=[whole_block(*ROW_TABLE)] * 2
        + [whole_block(*DECAY_TABLE), carried_block(STATE_HEADS, behind)],
        out_shape=[shape(ROW_TABLE, F32)] * 2
        + [shape(DECAY_TABLE, F32), shape(TRAVELLING, F32)],
        scratch_shapes=[pltpu.VMEM(ROW_TABLE, F32)],
        compiler_params=limit(60),
        name="states",
    )(layer_input, gate_weight.T, decay_rate, *heads)


def locals_of(running, *heads):
    return pl.pallas_call(
        local_kernel,
        grid=(HEADS // LOCAL_HEADS,),
        in_specs=[heads_block(LOCAL_HEADS)] * 4 + [whole_block(*ROW_TABLE)],
        out_specs=[flat_block(LOCAL_HEADS)] * 3
        + [turned_block(LOCAL_HEADS)] * 2
        + [whole_block(*ROW_TABLE)],
        out_shape=[shape((BLOCK, HEADS * DIM), F32)] * 3
        + [shape((HEADS * DIM, BLOCK), BF16)] * 2
        + [shape(ROW_TABLE, F32)],
        compiler_params=limit(60),
        name="locals",
    )(*heads, running)


def scanned(states):
    return pl.pallas_call(
        scan_kernel,
        grid=(PER,),
        in_specs=[pl.BlockSpec((GROUPS, ROWS, DIM), lambda i: (0, i, 0))],
        out_specs=pl.BlockSpec((GROUPS, ROWS, DIM), lambda i: (0, i, 0)),
        out_shape=shape((GROUPS, PER * ROWS, DIM), F32),
        compiler_params=limit(SCAN_MIB),
        name="scan",
    )(states)


def exchanged(array, axis="seq"):
    return lax.all_to_all(array, axis, 0, 0, tiled=True)


def terms_of(turned, pair, decay, carried, local_push, slope, layer_input):
    def ahead(i):
        return jnp.minimum(i, TERM_STEPS - 1)

    def beyond(i):
        return jnp.maximum(i - TERM_STEPS, 0)

    return pl.pallas_call(
        term_kernel,
        grid=(TERM_STEPS + GROUPS // TERM_OWNERS,),
        in_specs=[turned_block(TERM_HEADS, ahead)] * 2
        + [heads_block(TERM_HEADS, ahead)] * 2
        + [
            whole_block(*DECAY_TABLE),
            carried_block(TERM_HEADS, ahead),
            whole_block(*ROW_TABLE),
            whole_block(*ROW_TABLE),
            pl.BlockSpec((1, BLOCK, TERM_OWNERS * BLOCK), lambda i: (0, 0, beyond(i))),
        ],
        out_specs=pl.BlockSpec((TERM_OWNERS, HEADS, BLOCK), lambda i: (beyond(i), 0, 0)),
        out_shape=shape((GROUPS, HEADS, BLOCK), F32),
        scratch_shapes=[pltpu.VMEM(ROW_TABLE, F32)],
        compiler_params=limit(TERM_MIB),
        name="terms",
    )(*turned, *pair, decay, carried, local_push, slope, layer_input)


def query_key(value_heads, output_grad, decay, carried, query_local, key_local):
    return pl.pallas_call(
        query_kernel,
        grid=(HEADS // FULL_HEADS,),
        in_specs=[heads_block(FULL_HEADS)] * 2
        + [whole_block(*DECAY_TABLE), carried_block(FULL_HEADS)]
        + [flat_block(FULL_HEADS)] * 2,
        out_specs=[heads_block(FULL_HEADS)] * 2,
        out_shape=[shape(OUT, BF16)] * 2,
        compiler_params=limit(FULL_MIB),
        name="query_key",
    )(value_heads, output_grad, decay, carried, query_local, key_local)


def value_of(key_heads, decay, carried, value_local):
    return pl.pallas_call(
        value_kernel,
        grid=(HEADS // FULL_HEADS,),
        in_specs=[
            heads_block(FULL_HEADS),
            whole_block(*DECAY_TABLE),
            carried_block(FULL_HEADS),
            flat_block(FULL_HEADS),
        ],
        out_specs=heads_block(FULL_HEADS),
        out_shape=shape(OUT, BF16),
        compiler_params=limit(FULL_MIB),
        name="value",
    )(key_heads, decay, carried, value_local)


def after(array, *others):
    return lax.optimization_barrier((array, *others))[0]


def local(query_heads, key_heads, value_heads, output_grad, layer_input, gate_weight, decay_rate):
    heads = (query_heads, key_heads, value_heads, output_grad)
    running, slope, decay, states = states_of(layer_input, gate_weight, decay_rate, *heads)
    owned = exchanged(states.reshape(GROUPS, PER * ROWS, DIM))
    carried = exchanged(scanned(owned)).reshape(TRAVELLING)
    query_local, key_local, value_local, query_turned, key_turned, local_push = locals_of(
        running, *heads
    )
    pair = (value_heads, output_grad)
    terms = exchanged(
        terms_of((query_turned, key_turned), pair, decay, carried, local_push, slope, layer_input)
    )
    query_grad, key_grad = query_key(*pair, decay, carried, query_local, key_local)
    sums = jnp.sum(terms, axis=0)
    value_local = after(value_local, sums)
    sums = after(sums, query_grad)
    copies = jnp.broadcast_to(sums[None], (lax.axis_size("dp"),) + sums.shape)
    gathered = exchanged(copies, "dp")
    value_grad = value_of(key_heads, decay, carried, value_local)
    token_count = BLOCK * lax.axis_size("seq") * lax.axis_size("dp")
    weight_grad = jnp.sum(gathered, axis=0) / token_count
    return query_grad, key_grad, value_grad, weight_grad


def solution(mesh):
    heads = P("dp", "seq", None)
    return jax.shard_map(
        local,
        mesh=mesh,
        in_specs=(heads,) * 5 + (P(), P("dp", None, "seq")),
        out_specs=(heads,) * 3 + (P(None, "seq"),),
        check_vma=False,
    )
```

time: 682 us -> 188 us (0.28)
  waiting for transfers between devices: 442 us -> 35.5 us
  matrix products: 94.5 us -> 0 us
  Pallas kernels: 0 us -> 74 us
  local copies, waits for them, and re-layouts: 33.7 us -> 0.77 us
  other arithmetic: 31.4 us -> 0.7 us
  starting transfers between devices: 0.12 us -> 16.9 us
  between operations: 14.5 us -> 0.67 us
    all_gather x2 -> x0, waiting for transfers between devices: 309 us -> none  [carried_in(): gathered = jax.tree.map(lambda a: lax.all_gather(a, axis), part)]
    psum x1 -> x0, waiting for transfers between devices: 133 us -> none  [local(): summed = lax.psum(gate_term, ('dp', 'seq'))]
    dot_general x13 -> x0, matrix products: 94.5 us -> none  [the longest x1 17.3 us: local(): jnp.einsum('hts,thd->shd', mixing, query_rows, preferred_element_type=jnp...]
    pallas_call x0 -> x6, Pallas kernels: none -> 74 us  [the longest x1 25.8 us: locals_of(): pl.pallas_call(local_kernel, grid=(HEADS // LOCAL_HEADS,), in_specs=[head...]
    unnamed x2 -> x0, blocking collectives: 64 us -> none
    all_to_all x0 -> x1, blocking collectives: none -> 58.8 us  [exchanged(): return lax.all_to_all(array, axis, 0, 0, tiled=True)]
    all_to_all x0 -> x3, waiting for transfers between devices: none -> 35.5 us  [exchanged(): return lax.all_to_all(array, axis, 0, 0, tiled=True)]
    add x30 -> x0, other arithmetic: 29.9 us -> none  [the longest x15 29.6 us: combine(): later[0][:, None, None] * earlier[1] + later[1]]
  transfers between devices with their start and end apart: 3 -> 3, of which waited for: 3 -> 2; matrix products, arithmetic and copies ran while one was open for 11% -> 0% of each run, Pallas kernels for 0% -> 24%
where the time goes in v2:
time: 188 us; the launch traced here: 187 us
  Pallas kernels  74 us (39%)
  blocking collectives  58.8 us (31%)
  waiting for transfers between devices  35.5 us (19%)
  starting transfers between devices  16.9 us (9%)
    all_to_all x1, blocking collectives, exchanged(): return lax.all_to_all(array, axis, 0, 0, tiled=True)  58.8 us
    all_to_all x3, waiting for transfers between devices, exchanged(): return lax.all_to_all(array, axis, 0, 0, tiled=True)  35.5 us
    pallas_call x1, Pallas kernels, locals_of(): pl.pallas_call(local_kernel, grid=(HEADS // LOCAL_HEADS,), in_specs=[head...  25.8 us
    all_to_all x3, starting transfers between devices, exchanged(): return lax.all_to_all(array, axis, 0, 0, tiled=True)  16.9 us
    pallas_call x1, Pallas kernels, query_key(): pl.pallas_call(query_kernel, grid=(HEADS // FULL_HEADS,), in_specs=[heads...  12.2 us
    pallas_call x1, Pallas kernels, terms_of(): pl.pallas_call(term_kernel, grid=(TERM_STEPS + GROUPS // TERM_OWNERS,), i...  12.1 us
    pallas_call x1, Pallas kernels, states_of(): pl.pallas_call(state_kernel, grid=(GATE_STEPS + HEADS // STATE_HEADS,), i...  12 us
    pallas_call x1, Pallas kernels, value_of(): pl.pallas_call(value_kernel, grid=(HEADS // FULL_HEADS,), in_specs=[heads...  7.87 us
  transfers between devices with their start and end apart: 3, of which 2 were waited for; matrix products, arithmetic and copies ran while one was open for 0% of the time, Pallas kernels for 24%

profile of v2, /device:TPU:1, one launch (start us, length us, event | category | flops | bytes accessed | tf_op | source)
XLA Modules:
  0.0 187.3 jit_solution(4866331798988882450)
XLA Ops:
  0.6 12.0 %states.1 = (f32[32,384]{1,0:T(8,128)}, f32[32,384]{1,0:T(8,128)}, f32[64,384]{1,0:T(8,128)}, f32[32,264,128]{2,1,0:T(8,128)}) custom-call(bf16[1,384,6144]{2,1,0:T(8,128)(2,1)} %input_ref.3, bf16[32,6144]{1,0:T(8,128)(2,1)} %bitcast.4, f32[1,32,384]{2,1,0:T(8,128)} %rate_ref.1, bf16[1,384,4096]{2,1,0:T(8,128)(2,1)} %query_ref.3, ...), custom_call_target="tpu_custom_call" | custom-call | tf_op jit(solution)/shard_map/states/pallas_call | solution.py:256
  12.6 58.8 %all_to_all.20.states_ref = f32[16,528,128]{2,1,0:T(8,128)} all-to-all(f32[16,528,128]{2,1,0:T(8,128)} %bitcast.3), channel_id=1, replica_groups=mesh['dp'=8,'seq'=16] {'seq'}, dimensions={0} | all-to-all | bytes 8650752 | tf_op jit(solution)/shard_map/all_to_all | solution.py:304
  71.4 4.0 %scan.1 = f32[16,528,128]{2,1,0:T(8,128)} custom-call(f32[16,528,128]{2,1,0:T(8,128)} %all_to_all.20.states_ref), custom_call_target="tpu_custom_call" | custom-call | tf_op jit(solution)/shard_map/scan/pallas_call | solution.py:292
  75.5 4.6 %all-to-all-start.1 = ((f32[16,528,128]{2,1,0:T(8,128)}), f32[16,528,128]{2,1,0:T(8,128)}, u32[]{:S(2)}, u32[]{:S(2)}) async-start(f32[16,528,128]{2,1,0:T(8,128)} %scan.1), calls=%async_computation.1 | async-start | bytes 8650752 | tf_op jit(solution)/shard_map/all_to_all | solution.py:304
  80.1 25.8 %locals.1 = (f32[384,4096]{1,0:T(8,128)}, f32[384,4096]{1,0:T(8,128)}, f32[384,4096]{1,0:T(8,128)}, bf16[4096,384]{1,0:T(8,128)(2,1)}, bf16[4096,384]{1,0:T(8,128)(2,1)}, /*index=5*/f32[32,384]{1,0:T(8,128)}) custom-call(bf16[1,384,4096]{2,1,0:T(8,128)(2,1)} %query_ref.3, bf16[1,384,4096]{2,1,0:T(8,128)(2,1)} %key_ref.5, bf16[1,384,4096]{2,1,0:T(8,128)(2,1)} %value_ref.7, ...), custom_call_target="tpu_custom_call" | custom-call | tf_op jit(solution)/shard_map/locals/pallas_call | solution.py:276
  105.9 35.3 %all-to-all-done.1 = f32[16,528,128]{2,1,0:T(8,128)} async-done(((f32[16,528,128]{2,1,0:T(8,128)}), f32[16,528,128]{2,1,0:T(8,128)}, u32[]{:S(2)}, u32[]{:S(2)}) %all-to-all-start.1) | async-done | bytes 4325408 | tf_op jit(solution)/shard_map/all_to_all | solution.py:304
  141.1 12.1 %terms.1 = f32[16,32,384]{2,1,0:T(8,128)} custom-call(bf16[4096,384]{1,0:T(8,128)(2,1)} %get-tuple-element.26.query_ref, bf16[4096,384]{1,0:T(8,128)(2,1)} %get-tuple-element.27.key_ref, bf16[1,384,4096]{2,1,0:T(8,128)(2,1)} %value_ref.7, bf16[1,384,4096]{2,1,0:T(8,128)(2,1)} %grad_ref.7, f32[64,384]{1,0:T(8,128)} %get-tuple-element.18.decay_ref, ...), custom_call_target="tpu_custom_call" | custom-call | tf_op jit(solution)/shard_map/terms/pallas_call | solution.py:314
  153.2 3.8 %all-to-all-start.2 = ((f32[16,32,384]{2,1,0:T(8,128)}), f32[16,32,384]{2,1,0:T(8,128)S(1)}, u32[]{:S(2)}, u32[]{:S(2)}) async-start(f32[16,32,384]{2,1,0:T(8,128)} %terms.1), calls=%async_computation.2 | async-start | bytes 1572864 | tf_op jit(solution)/shard_map/all_to_all | solution.py:304
  157.0 12.2 %query_key.1 = (bf16[1,384,4096]{2,1,0:T(8,128)(2,1)}, bf16[1,384,4096]{2,1,0:T(8,128)(2,1)}) custom-call(bf16[1,384,4096]{2,1,0:T(8,128)(2,1)} %value_ref.7, bf16[1,384,4096]{2,1,0:T(8,128)(2,1)} %grad_ref.7, f32[64,384]{1,0:T(8,128)} %get-tuple-element.18.decay_ref, f32[32,264,128]{2,1,0:T(8,128)} %bitcast.2.carried_ref, ...), custom_call_target="tpu_custom_call" | custom-call | tf_op jit(solution)/shard_map/query_key/pallas_call | solution.py:335
  169.2 0.0 all-to-all-done.2
  169.3 0.8 broadcast_in_dim.2
  170.0 8.6 %all-to-all-start.3 = ((f32[8,32,384]{2,1,0:T(8,128)}), f32[8,32,384]{2,1,0:T(8,128)S(1)}, u32[]{:S(2)}, u32[]{:S(2)}) async-start(f32[8,32,384]{2,1,0:T(8,128)} %broadcast_in_dim.2), calls=%async_computation.3 | async-start | bytes 786432 | tf_op jit(solution)/shard_map/all_to_all | solution.py:304
  178.6 7.9 %value.1 = bf16[1,384,4096]{2,1,0:T(8,128)(2,1)} custom-call(bf16[1,384,4096]{2,1,0:T(8,128)(2,1)} %key_ref.5, f32[64,384]{1,0:T(8,128)} %get-tuple-element.18.decay_ref, f32[32,264,128]{2,1,0:T(8,128)} %bitcast.2.carried_ref, f32[384,4096]{1,0:T(8,128)} %get-tuple-element.30.vl_ref), custom_call_target="tpu_custom_call" | custom-call | tf_op jit(solution)/shard_map/value/pallas_call | solution.py:349
  186.5 0.2 all-to-all-done.3
  186.7 0.6 broadcast_multiply_fusion
  (2 shorter events, 0.1 us)
Async XLA Ops:
  75.5 65.6 %all-to-all-start.1 = ((f32[16,528,128]{2,1,0:T(8,128)}), f32[16,528,128]{2,1,0:T(8,128)}, u32[]{:S(2)}, u32[]{:S(2)}) async-start(f32[16,528,128]{2,1,0:T(8,128)} %scan.1), calls=%async_computation.1 | async-start | bytes 8650752 | tf_op jit(solution)/shard_map/all_to_all | solution.py:304
  153.2 16.0 %all-to-all-start.2 = ((f32[16,32,384]{2,1,0:T(8,128)}), f32[16,32,384]{2,1,0:T(8,128)S(1)}, u32[]{:S(2)}, u32[]{:S(2)}) async-start(f32[16,32,384]{2,1,0:T(8,128)} %terms.1), calls=%async_computation.2 | async-start | bytes 1572864 | tf_op jit(solution)/shard_map/all_to_all | solution.py:304
  170.0 16.6 %all-to-all-start.3 = ((f32[8,32,384]{2,1,0:T(8,128)}), f32[8,32,384]{2,1,0:T(8,128)S(1)}, u32[]{:S(2)}, u32[]{:S(2)}) async-start(f32[8,32,384]{2,1,0:T(8,128)} %broadcast_in_dim.2), calls=%async_computation.3 | async-start | bytes 786432 | tf_op jit(solution)/shard_map/all_to_all | solution.py:304

commit v3 on v2

--- a/solution.py
+++ b/solution.py
@@ -13,7 +13,7 @@
 MODEL = 6144
 GROUPS = 16
 PER = HEADS // GROUPS
-ROWS = 2 * DIM + 8
+ROWS = 2 * DIM * PER + 8
 SCALE = 1.0 / DIM
 GATE_STEP = 3072
 GATE_STEPS = MODEL // GATE_STEP
@@ -23,7 +23,6 @@
 TERM_STEPS = HEADS // TERM_HEADS
 FULL_HEADS = 8
 TERM_OWNERS = 8
-SCAN_MIB, TERM_MIB, FULL_MIB = 60, 60, 60
 
 
 def limit(mib):
@@ -48,6 +47,17 @@
     low = (rows - high.astype(F32)).astype(BF16)
     both = dot(ones, high, ((1,), (1,))) + dot(ones, low, ((1,), (1,)))
     return both[0:1]
+
+
+def travelling(head):
+    base = 2 * DIM * (head % PER)
+    own = 2 * DIM * PER + head % PER
+    return (
+        head // PER,
+        slice(base, base + DIM),
+        slice(base + DIM, base + 2 * DIM),
+        slice(own, own + 1),
+    )
 
 
 def state_kernel(
@@ -81,6 +91,7 @@
 
     @pl.when(step >= GATE_STEPS)
     def _():
+        out_ref[:, 2 * DIM * PER :, :] = jnp.zeros((STATE_HEADS // PER, 8, DIM), F32)
         for j in range(STATE_HEADS):
             cols = slice(j * DIM, (j + 1) * DIM)
             head = (step - GATE_STEPS) * STATE_HEADS + j
@@ -88,28 +99,40 @@
             to_end = decay_ref[pl.ds(HEADS + head, 1), :]
             key_faded = (key_ref[0, :, cols].T.astype(F32) * to_end).astype(BF16)
             query_faded = (query_ref[0, :, cols].T.astype(F32) * from_start).astype(BF16)
-            out_ref[j, :DIM, :] = dot(key_faded, value_ref[0, :, cols], ((1,), (0,)))
-            out_ref[j, DIM : 2 * DIM, :] = dot(query_faded, grad_ref[0, :, cols], ((1,), (0,)))
-            out_ref[j, 2 * DIM :, :] = jnp.broadcast_to(
-                from_start[:, BLOCK - 1 : BLOCK], (8, DIM)
-            )
-
-
-def scan_kernel(states_ref, out_ref):
-    early, late, own = slice(0, DIM), slice(DIM, 2 * DIM), slice(2 * DIM, 2 * DIM + 1)
-    prior = jnp.zeros((DIM, DIM), F32)
-    pushes = []
-    for n in range(GROUPS):
-        out_ref[n, :DIM, :] = prior
-        pushes.append(rounded_sum(prior, states_ref[n, late, :]))
-        prior = states_ref[n, early, :] + states_ref[n, own, :] * prior
-    later = jnp.zeros((DIM, DIM), F32)
-    tail = jnp.zeros((1, DIM), F32)
-    for n in reversed(range(GROUPS)):
-        out_ref[n, DIM : 2 * DIM, :] = later
-        out_ref[n, 2 * DIM :, :] = jnp.broadcast_to(tail, (8, DIM))
-        tail = tail + pushes[n] - rounded_sum(later, states_ref[n, early, :])
-        later = states_ref[n, late, :] + states_ref[n, own, :] * later
+            at, early, late, own = travelling(j)
+            out_ref[at, early, :] = dot(key_faded, value_ref[0, :, cols], ((1,), (0,)))
+            out_ref[at, late, :] = dot(query_faded, grad_ref[0, :, cols], ((1,), (0,)))
+            out_ref[at, own, :] = jnp.broadcast_to(from_start[:, BLOCK - 1 : BLOCK], (1, DIM))
+
+
+def scan_kernel(states_ref, rows_ref, out_ref, tails):
+    step = pl.program_id(0)
+    early, late = slice(0, DIM), slice(DIM, 2 * DIM)
+
+    @pl.when(step == 0)
+    def _():
+        tails[...] = jnp.zeros_like(tails)
+
+    @pl.when(step < PER)
+    def _():
+        own = pl.ds(step, 1)
+        prior = jnp.zeros((DIM, DIM), F32)
+        pushes = []
+        for n in range(GROUPS):
+            out_ref[n, early, :] = prior
+            pushes.append(rounded_sum(prior, states_ref[n, late, :]))
+            prior = states_ref[n, early, :] + rows_ref[n, own, :] * prior
+        later = jnp.zeros((DIM, DIM), F32)
+        tail = jnp.zeros((1, DIM), F32)
+        for n in reversed(range(GROUPS)):
+            out_ref[n, late, :] = later
+            tails[n, own, :] = tail
+            tail = tail + pushes[n] - rounded_sum(later, states_ref[n, early, :])
+            later = states_ref[n, late, :] + rows_ref[n, own, :] * later
+
+    @pl.when(step == PER)
+    def _():
+        out_ref[:, :8, :] = tails[...]
 
 
 def local_kernel(
@@ -133,9 +156,9 @@
         key_local = dot(mixing, query, ((0,), (0,)))
         qt_ref[cols, :] = query.T
         kt_ref[cols, :] = key.T
-        ql_ref[:, cols] = query_local
-        kl_ref[:, cols] = key_local
-        vl_ref[:, cols] = dot(weighted, grad, ((0,), (0,)))
+        ql_ref[:, cols] = query_local.astype(BF16)
+        kl_ref[:, cols] = key_local.astype(BF16)
+        vl_ref[:, cols] = dot(weighted, grad, ((0,), (0,))).astype(BF16)
         push_ref[head, :] = row_sums(
             query.astype(F32) * query_local - key.astype(F32) * key_local
         )
@@ -153,8 +176,9 @@
         for j in range(TERM_HEADS):
             head = step * TERM_HEADS + j
             cols = slice(j * DIM, (j + 1) * DIM)
-            prior = carried_ref[j, :DIM, :].astype(BF16)
-            later = carried_ref[j, DIM : 2 * DIM, :].astype(BF16)
+            at, early, late, own = travelling(j)
+            prior = carried_ref[at, early, :].astype(BF16)
+            later = carried_ref[at, late, :].astype(BF16)
             query_state = dot(prior, grad_ref[0, :, cols], ((1,), (1,)))
             key_state = dot(later, value_ref[0, :, cols], ((1,), (1,)))
             from_query = jnp.sum(
@@ -163,7 +187,7 @@
             from_key = jnp.sum(
                 key_ref[cols, :].astype(F32) * key_state, axis=0, keepdims=True
             ) * (decay_ref[pl.ds(HEADS + head, 1), :] * SCALE)
-            tail = jnp.sum(carried_ref[j, 2 * DIM : 2 * DIM + 1, :], axis=1, keepdims=True)
+            tail = jnp.sum(carried_ref[at, own, :], axis=1, keepdims=True)
             push[pl.ds(head, 1), :] = (
                 from_query - from_key + local_ref[pl.ds(head, 1), :] + jnp.where(last, tail, 0.0)
             )
@@ -186,33 +210,24 @@
             out_ref[i] = dot(logit_grad, input_ref[0, :, cols], ((1,), (0,)))
 
 
-def query_kernel(
-    value_ref, grad_ref, decay_ref, carried_ref, ql_ref, kl_ref, query_out, key_out
+def full_kernel(
+    key_ref, value_ref, grad_ref, decay_ref, carried_ref, ql_ref, kl_ref, vl_ref,
+    query_out, key_out, value_out,
 ):
     for j in range(FULL_HEADS):
         cols = slice(j * DIM, (j + 1) * DIM)
         head = pl.program_id(0) * FULL_HEADS + j
         from_start = as_column(decay_ref[pl.ds(head, 1), :] * SCALE)
         to_end = as_column(decay_ref[pl.ds(HEADS + head, 1), :] * SCALE)
-        prior = carried_ref[j, :DIM, :].astype(BF16)
-        later = carried_ref[j, DIM : 2 * DIM, :].astype(BF16)
-        query_out[0, :, cols] = (
-            ql_ref[:, cols] + from_start * dot(grad_ref[0, :, cols], prior, ((1,), (1,)))
-        ).astype(BF16)
-        key_out[0, :, cols] = (
-            kl_ref[:, cols] + to_end * dot(value_ref[0, :, cols], later, ((1,), (1,)))
-        ).astype(BF16)
-
-
-def value_kernel(key_ref, decay_ref, carried_ref, vl_ref, value_out):
-    for j in range(FULL_HEADS):
-        cols = slice(j * DIM, (j + 1) * DIM)
-        head = pl.program_id(0) * FULL_HEADS + j
-        to_end = as_column(decay_ref[pl.ds(HEADS + head, 1), :] * SCALE)
-        later = carried_ref[j, DIM : 2 * DIM, :].astype(BF16)
-        value_out[0, :, cols] = (
-            vl_ref[:, cols] + to_end * dot(key_ref[0, :, cols], later, ((1,), (0,)))
-        ).astype(BF16)
+        at, early, late, _ = travelling(j)
+        prior = carried_ref[at, early, :].astype(BF16)
+        later = carried_ref[at, late, :].astype(BF16)
+        query_state = from_start * dot(grad_ref[0, :, cols], prior, ((1,), (1,)))
+        key_state = to_end * dot(value_ref[0, :, cols], later, ((1,), (1,)))
+        value_state = to_end * dot(key_ref[0, :, cols], later, ((1,), (0,)))
+        query_out[0, :, cols] = (ql_ref[:, cols].astype(F32) + query_state).astype(BF16)
+        key_out[0, :, cols] = (kl_ref[:, cols].astype(F32) + key_state).astype(BF16)
+        value_out[0, :, cols] = (vl_ref[:, cols].astype(F32) + value_state).astype(BF16)
 
 
 def same(i):
@@ -224,7 +239,7 @@
 
 
 def carried_block(heads, group=same):
-    return pl.BlockSpec((heads, ROWS, DIM), lambda i: (group(i), 0, 0))
+    return pl.BlockSpec((heads // PER, ROWS, DIM), lambda i: (group(i), 0, 0))
 
 
 def flat_block(heads, group=same):
@@ -242,7 +257,8 @@
 shape = jax.ShapeDtypeStruct
 ROW_TABLE = (HEADS, BLOCK)
 DECAY_TABLE = (2 * HEADS, BLOCK)
-TRAVELLING = (HEADS, ROWS, DIM)
+TRAVELLING = (GROUPS, ROWS, DIM)
+FLAT = (BLOCK, HEADS * DIM)
 OUT = (1, BLOCK, HEADS * DIM)
 
 
@@ -280,28 +296,53 @@
         out_specs=[flat_block(LOCAL_HEADS)] * 3
         + [turned_block(LOCAL_HEADS)] * 2
         + [whole_block(*ROW_TABLE)],
-        out_shape=[shape((BLOCK, HEADS * DIM), F32)] * 3
-        + [shape((HEADS * DIM, BLOCK), BF16)] * 2
+        out_shape=[pltpu.HBM(FLAT, BF16)] * 3
+        + [pltpu.HBM((HEADS * DIM, BLOCK), BF16)] * 2
         + [shape(ROW_TABLE, F32)],
-        compiler_params=limit(60),
+        compiler_params=limit(48),
         name="locals",
-    )(*heads, running)
+    )(*in_hbm(*heads), running)
 
 
 def scanned(states):
+    def ahead(i):
+        return jnp.minimum(i, PER - 1)
+
     return pl.pallas_call(
         scan_kernel,
-        grid=(PER,),
-        in_specs=[pl.BlockSpec((GROUPS, ROWS, DIM), lambda i: (0, i, 0))],
-        out_specs=pl.BlockSpec((GROUPS, ROWS, DIM), lambda i: (0, i, 0)),
-        out_shape=shape((GROUPS, PER * ROWS, DIM), F32),
-        compiler_params=limit(SCAN_MIB),
+        grid=(PER + 1,),
+        in_specs=[
+            pl.BlockSpec((GROUPS, 2 * DIM, DIM), lambda i: (0, ahead(i), 0)),
+            pl.BlockSpec((GROUPS, 8, DIM), lambda i: (0, 2 * DIM * PER // 8, 0)),
+        ],
+        out_specs=pl.BlockSpec((GROUPS, 2 * DIM, DIM), lambda i: (0, i, 0)),
+        out_shape=pltpu.HBM(TRAVELLING, F32),
+        scratch_shapes=[pltpu.VMEM((GROUPS, 8, DIM), F32)],
+        compiler_params=limit(32),
         name="scan",
-    )(states)
+    )(in_vmem(states), in_vmem(states))
 
 
 def exchanged(array, axis="seq"):
     return lax.all_to_all(array, axis, 0, 0, tiled=True)
+
+
+def in_hbm(*arrays):
+    return [pltpu.with_memory_space_constraint(array, pltpu.HBM) for array in arrays]
+
+
+def in_vmem(array):
+    return pltpu.with_memory_space_constraint(array, pltpu.VMEM)
+
+
+def summed_over_dp(part):
+    count = lax.axis_size("dp")
+    pair = part + lax.ppermute(part, "dp", [(i, i ^ 1) for i in range(count)])
+    first, second, third = (
+        lax.ppermute(pair, "dp", [(i, (i + 2 * step) % count) for i in range(count)])
+        for step in (1, 2, 3)
+    )
+    return (pair + second) + (first + third)
 
 
 def terms_of(turned, pair, decay, carried, local_push, slope, layer_input):
@@ -324,42 +365,27 @@
             pl.BlockSpec((1, BLOCK, TERM_OWNERS * BLOCK), lambda i: (0, 0, beyond(i))),
         ],
         out_specs=pl.BlockSpec((TERM_OWNERS, HEADS, BLOCK), lambda i: (beyond(i), 0, 0)),
-        out_shape=shape((GROUPS, HEADS, BLOCK), F32),
+        out_shape=pltpu.HBM((GROUPS, HEADS, BLOCK), F32),
         scratch_shapes=[pltpu.VMEM(ROW_TABLE, F32)],
-        compiler_params=limit(TERM_MIB),
+        compiler_params=limit(48),
         name="terms",
-    )(*turned, *pair, decay, carried, local_push, slope, layer_input)
-
-
-def query_key(value_heads, output_grad, decay, carried, query_local, key_local):
+    )(
+        *in_hbm(*turned, *pair), decay, in_vmem(carried), local_push, slope, *in_hbm(layer_input)
+    )
+
+
+def full_of(heads, decay, carried, *local_parts):
     return pl.pallas_call(
-        query_kernel,
+        full_kernel,
         grid=(HEADS // FULL_HEADS,),
-        in_specs=[heads_block(FULL_HEADS)] * 2
+        in_specs=[heads_block(FULL_HEADS)] * 3
         + [whole_block(*DECAY_TABLE), carried_block(FULL_HEADS)]
-        + [flat_block(FULL_HEADS)] * 2,
-        out_specs=[heads_block(FULL_HEADS)] * 2,
-        out_shape=[shape(OUT, BF16)] * 2,
-        compiler_params=limit(FULL_MIB),
-        name="query_key",
-    )(value_heads, output_grad, decay, carried, query_local, key_local)
-
-
-def value_of(key_heads, decay, carried, value_local):
-    return pl.pallas_call(
-        value_kernel,
-        grid=(HEADS // FULL_HEADS,),
-        in_specs=[
-            heads_block(FULL_HEADS),
-            whole_block(*DECAY_TABLE),
-            carried_block(FULL_HEADS),
-            flat_block(FULL_HEADS),
-        ],
-        out_specs=heads_block(FULL_HEADS),
-        out_shape=shape(OUT, BF16),
-        compiler_params=limit(FULL_MIB),
-        name="value",
-    )(key_heads, decay, carried, value_local)
+        + [flat_block(FULL_HEADS)] * 3,
+        out_specs=[heads_block(FULL_HEADS)] * 3,
+        out_shape=[shape(OUT, BF16)] * 3,
+        compiler_params=limit(48),
+        name="full",
+    )(*in_hbm(*heads), decay, in_vmem(carried), *in_hbm(*local_parts))
 
 
 def after(array, *others):
@@ -369,25 +395,17 @@
 def local(query_heads, key_heads, value_heads, output_grad, layer_input, gate_weight, decay_rate):
     heads = (query_heads, key_heads, value_heads, output_grad)
     running, slope, decay, states = states_of(layer_input, gate_weight, decay_rate, *heads)
-    owned = exchanged(states.reshape(GROUPS, PER * ROWS, DIM))
-    carried = exchanged(scanned(owned)).reshape(TRAVELLING)
-    query_local, key_local, value_local, query_turned, key_turned, local_push = locals_of(
-        running, *heads
+    carried = exchanged(scanned(exchanged(states)))
+    *local_parts, query_turned, key_turned, local_push = locals_of(running, *heads)
+    turned = (query_turned, key_turned)
+    terms = exchanged(
+        terms_of(turned, heads[2:], decay, carried, local_push, slope, layer_input)
     )
-    pair = (value_heads, output_grad)
-    terms = exchanged(
-        terms_of((query_turned, key_turned), pair, decay, carried, local_push, slope, layer_input)
-    )
-    query_grad, key_grad = query_key(*pair, decay, carried, query_local, key_local)
-    sums = jnp.sum(terms, axis=0)
-    value_local = after(value_local, sums)
-    sums = after(sums, query_grad)
-    copies = jnp.broadcast_to(sums[None], (lax.axis_size("dp"),) + sums.shape)
-    gathered = exchanged(copies, "dp")
-    value_grad = value_of(key_heads, decay, carried, value_local)
+    grads = full_of(heads[1:], decay, carried, *local_parts)
+    sums = after(jnp.sum(terms, axis=0), grads[0])
     token_count = BLOCK * lax.axis_size("seq") * lax.axis_size("dp")
-    weight_grad = jnp.sum(gathered, axis=0) / token_count
-    return query_grad, key_grad, value_grad, weight_grad
+    weight_grad = summed_over_dp(sums) / token_count
+    return *grads, weight_grad
 
 
 def solution(mesh):

time: 188 us -> 181 us (0.963)
  Pallas kernels: 74 us -> 63.7 us
  waiting for transfers between devices: 35.5 us -> 38.3 us
    ppermute x0 -> x4, starting transfers between devices: none -> 9.49 us  [the longest x3 6.31 us: summed_over_dp(): lax.ppermute(pair, 'dp', [(i, (i + 2 * step) % count) for i in range(coun...]
    pallas_call x3 -> x2, Pallas kernels: 24.1 us -> 15.5 us  [the longest x1 12.7 us: full_of(): pl.pallas_call(full_kernel, grid=(HEADS // FULL_HEADS,), in_specs=[heads_...]
    all_to_all x3 -> x2, starting transfers between devices: 16.9 us -> 8.66 us  [exchanged(): return lax.all_to_all(array, axis, 0, 0, tiled=True)]
    ppermute x0 -> x4, waiting for transfers between devices: none -> 2.36 us  [the longest x3 1.48 us: summed_over_dp(): lax.ppermute(pair, 'dp', [(i, (i + 2 * step) % count) for i in range(coun...]
    all_to_all x3 -> x2, waiting for transfers between devices: 35.5 us -> 35.9 us  [exchanged(): return lax.all_to_all(array, axis, 0, 0, tiled=True)]
  transfers between devices with their start and end apart: 3 -> 6, of which waited for: 2 -> 3; matrix products, arithmetic and copies ran while one was open for 0% -> 0% of each run, Pallas kernels for 24% -> 21%
where the time goes in v3:
time: 181 us; the launch traced here: 180 us
  Pallas kernels  63.7 us (35%)
  blocking collectives  58.2 us (32%)
  waiting for transfers between devices  38.3 us (21%)
  starting transfers between devices  18.1 us (10%)
    all_to_all x1, blocking collectives, exchanged(): return lax.all_to_all(array, axis, 0, 0, tiled=True)  58.2 us
    all_to_all x2, waiting for transfers between devices, exchanged(): return lax.all_to_all(array, axis, 0, 0, tiled=True)  35.9 us
    pallas_call x1, Pallas kernels, locals_of(): pl.pallas_call(local_kernel, grid=(HEADS // LOCAL_HEADS,), in_specs=[head...  24.5 us
    pallas_call x1, Pallas kernels, full_of(): pl.pallas_call(full_kernel, grid=(HEADS // FULL_HEADS,), in_specs=[heads_...  12.7 us
    pallas_call x1, Pallas kernels, states_of(): pl.pallas_call(state_kernel, grid=(GATE_STEPS + HEADS // STATE_HEADS,), i...  12 us
    pallas_call x1, Pallas kernels, terms_of(): pl.pallas_call(term_kernel, grid=(TERM_STEPS + GROUPS // TERM_OWNERS,), i...  11.7 us
    all_to_all x2, starting transfers between devices, exchanged(): return lax.all_to_all(array, axis, 0, 0, tiled=True)  8.66 us
    ppermute x3, starting transfers between devices, summed_over_dp(): lax.ppermute(pair, 'dp', [(i, (i + 2 * step) % count) for i in range(coun...  6.31 us
  transfers between devices with their start and end apart: 6, of which 3 were waited for; matrix products, arithmetic and copies ran while one was open for 0% of the time, Pallas kernels for 21%

profile of v3, /device:TPU:1, one launch (start us, length us, event | category | flops | bytes accessed | tf_op | source)
XLA Modules:
  0.0 179.7 jit_solution(17115094250361568743)
XLA Ops:
  0.6 12.0 %states.1 = (f32[32,384]{1,0:T(8,128)}, f32[32,384]{1,0:T(8,128)}, f32[64,384]{1,0:T(8,128)}, f32[16,520,128]{2,1,0:T(8,128)}) custom-call(bf16[1,384,6144]{2,1,0:T(8,128)(2,1)} %input_ref.3, bf16[32,6144]{1,0:T(8,128)(2,1)} %bitcast.1, f32[1,32,384]{2,1,0:T(8,128)} %rate_ref.1, bf16[1,384,4096]{2,1,0:T(8,128)(2,1)} %query_ref.3, ...), custom_call_target="tpu_custom_call" | custom-call | tf_op jit(solution)/shard_map/states/pallas_call | solution.py:272
  12.6 58.2 %all_to_all.15.states_ref.rows_ref = f32[16,520,128]{2,1,0:T(8,128)S(1)} all-to-all(f32[16,520,128]{2,1,0:T(8,128)} %get-tuple-element.19), channel_id=1, replica_groups=mesh['dp'=8,'seq'=16] {'seq'}, dimensions={0} | all-to-all | bytes 8519680 | tf_op jit(solution)/shard_map/all_to_all | solution.py:327
  70.8 2.8 %scan.1 = f32[16,520,128]{2,1,0:T(8,128)} custom-call(f32[16,520,128]{2,1,0:T(8,128)S(1)} %all_to_all.15.states_ref.rows_ref, f32[16,520,128]{2,1,0:T(8,128)S(1)} %all_to_all.15.states_ref.rows_ref), custom_call_target="tpu_custom_call" | custom-call | tf_op jit(solution)/shard_map/scan/pallas_call | solution.py:311
  73.5 0.0 copy-start.1
  73.6 4.7 %all-to-all-start.1 = ((f32[16,520,128]{2,1,0:T(8,128)}), f32[16,520,128]{2,1,0:T(8,128)}, u32[]{:S(2)}, u32[]{:S(2)}) async-start(f32[16,520,128]{2,1,0:T(8,128)} %scan.1), calls=%async_computation.1 | async-start | bytes 8519680 | tf_op jit(solution)/shard_map/all_to_all | solution.py:327
  78.2 0.0 copy-done.1
  78.2 0.0 copy-start
  78.3 0.0 copy-start.2
  78.3 24.5 %locals.1 = (bf16[384,4096]{1,0:T(8,128)(2,1)}, bf16[384,4096]{1,0:T(8,128)(2,1)}, bf16[384,4096]{1,0:T(8,128)(2,1)}, bf16[4096,384]{1,0:T(8,128)(2,1)}, bf16[40...) custom-call(bf16[1,384,4096]{2,1,0:T(8,128)(2,1)} %query_ref.3, bf16[1,384,4096]{2,1,0:T(8,128)(2,1)} %key_ref.5, ...), custom_call_target="tpu_custom_call" | custom-call | tf_op jit(solution)/shard_map/locals/pallas_call | solution.py:292
  102.7 35.9 %all-to-all-done.1.carried_ref = f32[16,520,128]{2,1,0:T(8,128)} async-done(((f32[16,520,128]{2,1,0:T(8,128)}), f32[16,520,128]{2,1,0:T(8,128)}, u32[]{:S(2)}, u32[]{:S(2)}) %all-to-all-start.1) | async-done | bytes 4259872 | tf_op jit(solution)/shard_map/all_to_all | solution.py:327
  138.7 0.0 copy-done
  138.7 0.0 copy-done.2
  138.7 11.7 %terms.1 = f32[16,32,384]{2,1,0:T(8,128)} custom-call(bf16[4096,384]{1,0:T(8,128)(2,1)} %get-tuple-element.27.query_ref, bf16[4096,384]{1,0:T(8,128)(2,1)} %get-tuple-element.28.key_ref, bf16[1,384,4096]{2,1,0:T(8,128)(2,1)} %value_ref.7, bf16[1,384,4096]{2,1,0:T(8,128)(2,1)} %grad_ref.7, f32[64,384]{1,0:T(8,128)S(1)} %copy-done, ...), custom_call_target="tpu_custom_call" | custom-call | tf_op jit(solution)/shard_map/terms/pallas_call | solution.py:355
  150.4 4.0 %all-to-all-start.2 = ((f32[16,32,384]{2,1,0:T(8,128)}), f32[16,32,384]{2,1,0:T(8,128)S(1)}, u32[]{:S(2)}, u32[]{:S(2)}) async-start(f32[16,32,384]{2,1,0:T(8,128)} %terms.1), calls=%async_computation.2 | async-start | bytes 1572864 | tf_op jit(solution)/shard_map/all_to_all | solution.py:327
  154.4 12.7 %full.1 = (bf16[1,384,4096]{2,1,0:T(8,128)(2,1)}, bf16[1,384,4096]{2,1,0:T(8,128)(2,1)}, bf16[1,384,4096]{2,1,0:T(8,128)(2,1)}) custom-call(bf16[1,384,4096]{2,1,0:T(8,128)(2,1)} %key_ref.5, bf16[1,384,4096]{2,1,0:T(8,128)(2,1)} %value_ref.7, bf16[1,384,4096]{2,1,0:T(8,128)(2,1)} %grad_ref.7, f32[64,384]{1,0:T(8,128)S(1)} %copy-done, ...), custom_call_target="tpu_custom_call" | custom-call | tf_op jit(solution)/shard_map/full/pallas_call | solution.py:378
  167.1 0.0 all-to-all-done.2
  167.2 3.2 %collective-permute-start = (f32[32,384]{1,0:T(8,128)S(1)}, f32[32,384]{1,0:T(8,128)S(1)}, u32[]{:S(2)}, u32[]{:S(2)}) collective-permute-start(f32[32,384]{1,0:T(8,128)S(1)} %reduce_sum.9), channel_id=1, source_target_pairs={{0,16},{16,0},{32,48},{48,32},{64,80},{80,64},{96,112},{112,96},{1... | collective-permute-start | bytes 147464 | tf_op jit(solution)/shard_map/ppermute | solution.py:340
  170.4 0.9 collective-permute-done
  171.3 3.6 %collective-permute-start.1 = (f32[32,384]{1,0:T(8,128)S(1)}, f32[32,384]{1,0:T(8,128)S(1)}, u32[]{:S(2)}, u32[]{:S(2)}) collective-permute-start(f32[32,384]{1,0:T(8,128)S(1)} %add.12), channel_id=1, source_target_pairs={{0,64},{16,80},{32,96},{48,112},{64,0},{80,16},{96,32},{112,48},{1... | collective-permute-start | bytes 147464 | tf_op jit(solution)/shard_map/ppermute | solution.py:342
  174.9 0.7 collective-permute-start.2
  175.6 1.9 %collective-permute-start.3 = (f32[32,384]{1,0:T(8,128)S(1)}, f32[32,384]{1,0:T(8,128)S(1)}, u32[]{:S(2)}, u32[]{:S(2)}) collective-permute-start(f32[32,384]{1,0:T(8,128)S(1)} %add.12), channel_id=1, source_target_pairs={{0,96},{16,112},{32,0},{48,16},{64,32},{80,48},{96,64},{112,80},{1... | collective-permute-start | bytes 147464 | tf_op jit(solution)/shard_map/ppermute | solution.py:342
  177.6 0.0 collective-permute-done.1
  177.6 1.5 collective-permute-done.2
  179.0 0.0 collective-permute-done.3
  179.1 0.6 add_multiply_fusion
  (2 shorter events, 0.1 us)
Async XLA Ops:
  73.5 4.7 %copy-start.1 = (f32[32,384]{1,0:T(8,128)S(1)}, f32[32,384]{1,0:T(8,128)}, u32[]{:S(2)}) copy-start(f32[32,384]{1,0:T(8,128)} %get-tuple-element.20.running_ref) | copy-start | bytes 147460
  73.6 65.1 %all-to-all-start.1 = ((f32[16,520,128]{2,1,0:T(8,128)}), f32[16,520,128]{2,1,0:T(8,128)}, u32[]{:S(2)}, u32[]{:S(2)}) async-start(f32[16,520,128]{2,1,0:T(8,128)} %scan.1), calls=%async_computation.1 | async-start | bytes 8519680 | tf_op jit(solution)/shard_map/all_to_all | solution.py:327
  78.2 60.4 %copy-start = (f32[64,384]{1,0:T(8,128)S(1)}, f32[64,384]{1,0:T(8,128)}, u32[]{:S(2)}) copy-start(f32[64,384]{1,0:T(8,128)} %get-tuple-element.18.decay_ref) | copy-start | bytes 294916
  78.3 60.4 %copy-start.2 = (f32[32,384]{1,0:T(8,128)S(1)}, f32[32,384]{1,0:T(8,128)}, u32[]{:S(2)}) copy-start(f32[32,384]{1,0:T(8,128)} %get-tuple-element.30.slope_ref) | copy-start | bytes 147460
  150.4 16.7 %all-to-all-start.2 = ((f32[16,32,384]{2,1,0:T(8,128)}), f32[16,32,384]{2,1,0:T(8,128)S(1)}, u32[]{:S(2)}, u32[]{:S(2)}) async-start(f32[16,32,384]{2,1,0:T(8,128)} %terms.1), calls=%async_computation.2 | async-start | bytes 1572864 | tf_op jit(solution)/shard_map/all_to_all | solution.py:327
  167.2 4.1 %collective-permute-start = (f32[32,384]{1,0:T(8,128)S(1)}, f32[32,384]{1,0:T(8,128)S(1)}, u32[]{:S(2)}, u32[]{:S(2)}) collective-permute-start(f32[32,384]{1,0:T(8,128)S(1)} %reduce_sum.9), channel_id=1, source_target_pairs={{0,16},{16,0},{32,48},{48,32},{64,80},{80,64},{96,112},{112,96},{1... | collective-permute-start | bytes 147464 | tf_op jit(solution)/shard_map/ppermute | solution.py:340
  171.3 6.3 %collective-permute-start.1 = (f32[32,384]{1,0:T(8,128)S(1)}, f32[32,384]{1,0:T(8,128)S(1)}, u32[]{:S(2)}, u32[]{:S(2)}) collective-permute-start(f32[32,384]{1,0:T(8,128)S(1)} %add.12), channel_id=1, source_target_pairs={{0,64},{16,80},{32,96},{48,112},{64,0},{80,16},{96,32},{112,48},{1... | collective-permute-start | bytes 147464 | tf_op jit(solution)/shard_map/ppermute | solution.py:342
  174.9 4.2 %collective-permute-start.2 = (f32[32,384]{1,0:T(8,128)S(1)}, f32[32,384]{1,0:T(8,128)S(1)}, u32[]{:S(2)}, u32[]{:S(2)}) collective-permute-start(f32[32,384]{1,0:T(8,128)S(1)} %add.12), channel_id=1, source_target_pairs={{0,32},{16,48},{32,64},{48,80},{64,96},{80,112},{96,0},{112,16},{1... | collective-permute-start | bytes 147464 | tf_op jit(solution)/shard_map/ppermute | solution.py:342
  175.6 3.4 %collective-permute-start.3 = (f32[32,384]{1,0:T(8,128)S(1)}, f32[32,384]{1,0:T(8,128)S(1)}, u32[]{:S(2)}, u32[]{:S(2)}) collective-permute-start(f32[32,384]{1,0:T(8,128)S(1)} %add.12), channel_id=1, source_target_pairs={{0,96},{16,112},{32,0},{48,16},{64,32},{80,48},{96,64},{112,80},{1... | collective-permute-start | bytes 147464 | tf_op jit(solution)/shard_map/ppermute | solution.py:342

commit v4 on v3

--- a/solution.py
+++ b/solution.py
@@ -15,8 +15,8 @@
 PER = HEADS // GROUPS
 ROWS = 2 * DIM * PER + 8
 SCALE = 1.0 / DIM
-GATE_STEP = 3072
-GATE_STEPS = MODEL // GATE_STEP
+GATE_STEP = 128
+GATE_STEPS = BLOCK // GATE_STEP
 STATE_HEADS = 8
 LOCAL_HEADS = 2
 TERM_HEADS = 8
@@ -66,13 +66,10 @@
 ):
     step = pl.program_id(0)
 
-    @pl.when(step == 0)
-    def _():
-        logits[...] = dot(weight_ref[...], input_ref[0], ((1,), (1,)))
-
-    @pl.when((step > 0) & (step < GATE_STEPS))
-    def _():
-        logits[...] += dot(weight_ref[...], input_ref[0], ((1,), (1,)))
+    @pl.when(step < GATE_STEPS)
+    def _():
+        cols = pl.ds(pl.multiple_of(step * GATE_STEP, GATE_STEP), GATE_STEP)
+        logits[:, cols] = dot(weight_ref[...], input_ref[0], ((1,), (1,)))
 
     @pl.when(step == GATE_STEPS - 1)
     def _():
@@ -263,7 +260,7 @@
 
 
 def states_of(layer_input, gate_weight, decay_rate, *heads):
-    def feature(i):
+    def position(i):
         return jnp.minimum(i, GATE_STEPS - 1)
 
     def behind(i):
@@ -273,8 +270,8 @@
         state_kernel,
         grid=(GATE_STEPS + HEADS // STATE_HEADS,),
         in_specs=[
-            pl.BlockSpec((1, BLOCK, GATE_STEP), lambda i: (0, 0, feature(i))),
-            pl.BlockSpec((HEADS, GATE_STEP), lambda i: (0, feature(i))),
+            pl.BlockSpec((1, GATE_STEP, MODEL), lambda i: (0, position(i), 0)),
+            whole_block(HEADS, MODEL),
             whole_block(1, HEADS, BLOCK),
         ]
         + [heads_block(STATE_HEADS, behind)] * 4,
@@ -299,7 +296,7 @@
         out_shape=[pltpu.HBM(FLAT, BF16)] * 3
         + [pltpu.HBM((HEADS * DIM, BLOCK), BF16)] * 2
         + [shape(ROW_TABLE, F32)],
-        compiler_params=limit(48),
+        compiler_params=limit(30),
         name="locals",
     )(*in_hbm(*heads), running)
 
@@ -367,7 +364,7 @@
         out_specs=pl.BlockSpec((TERM_OWNERS, HEADS, BLOCK), lambda i: (beyond(i), 0, 0)),
         out_shape=pltpu.HBM((GROUPS, HEADS, BLOCK), F32),
         scratch_shapes=[pltpu.VMEM(ROW_TABLE, F32)],
-        compiler_params=limit(48),
+        compiler_params=limit(30),
         name="terms",
     )(
         *in_hbm(*turned, *pair), decay, in_vmem(carried), local_push, slope, *in_hbm(layer_input)
@@ -383,7 +380,7 @@
         + [flat_block(FULL_HEADS)] * 3,
         out_specs=[heads_block(FULL_HEADS)] * 3,
         out_shape=[shape(OUT, BF16)] * 3,
-        compiler_params=limit(48),
+        compiler_params=limit(30),
         name="full",
     )(*in_hbm(*heads), decay, in_vmem(carried), *in_hbm(*local_parts))
 

time: 181 us -> 182 us (level)
  no operation moved by 1% of the time
where the time goes in v4:
time: 182 us; the launch traced here: 180 us
  Pallas kernels  64.4 us (35%)
  blocking collectives  58.2 us (32%)
  waiting for transfers between devices  38.3 us (21%)
  starting transfers between devices  18.2 us (10%)
    all_to_all x1, blocking collectives, exchanged(): return lax.all_to_all(array, axis, 0, 0, tiled=True)  58.2 us
    all_to_all x2, waiting for transfers between devices, exchanged(): return lax.all_to_all(array, axis, 0, 0, tiled=True)  35.9 us
    pallas_call x1, Pallas kernels, locals_of(): pl.pallas_call(local_kernel, grid=(HEADS // LOCAL_HEADS,), in_specs=[head...  24.5 us
    pallas_call x1, Pallas kernels, states_of(): pl.pallas_call(state_kernel, grid=(GATE_STEPS + HEADS // STATE_HEADS,), i...  12.7 us
    pallas_call x1, Pallas kernels, full_of(): pl.pallas_call(full_kernel, grid=(HEADS // FULL_HEADS,), in_specs=[heads_...  12.7 us
    pallas_call x1, Pallas kernels, terms_of(): pl.pallas_call(term_kernel, grid=(TERM_STEPS + GROUPS // TERM_OWNERS,), i...  11.7 us
    all_to_all x2, starting transfers between devices, exchanged(): return lax.all_to_all(array, axis, 0, 0, tiled=True)  8.66 us
    ppermute x3, starting transfers between devices, summed_over_dp(): lax.ppermute(pair, 'dp', [(i, (i + 2 * step) % count) for i in range(coun...  6.31 us
  transfers between devices with their start and end apart: 6, of which 3 were waited for; matrix products, arithmetic and copies ran while one was open for 0% of the time, Pallas kernels for 21%

profile of v4, /device:TPU:1, one launch (start us, length us, event | category | flops | bytes accessed | tf_op | source)
XLA Modules:
  0.0 180.5 jit_solution(3390992175285366125)
XLA Ops:
  0.6 12.7 %states.1 = (f32[32,384]{1,0:T(8,128)}, f32[32,384]{1,0:T(8,128)}, f32[64,384]{1,0:T(8,128)}, f32[16,520,128]{2,1,0:T(8,128)}) custom-call(bf16[1,384,6144]{2,1,0:T(8,128)(2,1)} %input_ref.3, bf16[32,6144]{1,0:T(8,128)(2,1)} %bitcast.1, f32[1,32,384]{2,1,0:T(8,128)} %rate_ref.1, bf16[1,384,4096]{2,1,0:T(8,128)(2,1)} %query_ref.3, ...), custom_call_target="tpu_custom_call" | custom-call | tf_op jit(solution)/shard_map/states/pallas_call | solution.py:269
  13.4 58.2 %all_to_all.15.states_ref.rows_ref = f32[16,520,128]{2,1,0:T(8,128)S(1)} all-to-all(f32[16,520,128]{2,1,0:T(8,128)} %get-tuple-element.19), channel_id=1, replica_groups=mesh['dp'=8,'seq'=16] {'seq'}, dimensions={0} | all-to-all | bytes 8519680 | tf_op jit(solution)/shard_map/all_to_all | solution.py:324
  71.6 2.8 %scan.1 = f32[16,520,128]{2,1,0:T(8,128)} custom-call(f32[16,520,128]{2,1,0:T(8,128)S(1)} %all_to_all.15.states_ref.rows_ref, f32[16,520,128]{2,1,0:T(8,128)S(1)} %all_to_all.15.states_ref.rows_ref), custom_call_target="tpu_custom_call" | custom-call | tf_op jit(solution)/shard_map/scan/pallas_call | solution.py:308
  74.3 0.0 copy-start.1
  74.3 4.7 %all-to-all-start.1 = ((f32[16,520,128]{2,1,0:T(8,128)}), f32[16,520,128]{2,1,0:T(8,128)}, u32[]{:S(2)}, u32[]{:S(2)}) async-start(f32[16,520,128]{2,1,0:T(8,128)} %scan.1), calls=%async_computation.1 | async-start | bytes 8519680 | tf_op jit(solution)/shard_map/all_to_all | solution.py:324
  79.0 0.0 copy-done.1
  79.0 0.0 copy-start
  79.0 0.0 copy-start.2
  79.0 24.5 %locals.1 = (bf16[384,4096]{1,0:T(8,128)(2,1)}, bf16[384,4096]{1,0:T(8,128)(2,1)}, bf16[384,4096]{1,0:T(8,128)(2,1)}, bf16[4096,384]{1,0:T(8,128)(2,1)}, bf16[40...) custom-call(bf16[1,384,4096]{2,1,0:T(8,128)(2,1)} %query_ref.3, bf16[1,384,4096]{2,1,0:T(8,128)(2,1)} %key_ref.5, ...), custom_call_target="tpu_custom_call" | custom-call | tf_op jit(solution)/shard_map/locals/pallas_call | solution.py:289
  103.5 35.9 %all-to-all-done.1.carried_ref = f32[16,520,128]{2,1,0:T(8,128)} async-done(((f32[16,520,128]{2,1,0:T(8,128)}), f32[16,520,128]{2,1,0:T(8,128)}, u32[]{:S(2)}, u32[]{:S(2)}) %all-to-all-start.1) | async-done | bytes 4259872 | tf_op jit(solution)/shard_map/all_to_all | solution.py:324
  139.4 0.0 copy-done
  139.4 0.0 copy-done.2
  139.4 11.7 %terms.1 = f32[16,32,384]{2,1,0:T(8,128)} custom-call(bf16[4096,384]{1,0:T(8,128)(2,1)} %get-tuple-element.27.query_ref, bf16[4096,384]{1,0:T(8,128)(2,1)} %get-tuple-element.28.key_ref, bf16[1,384,4096]{2,1,0:T(8,128)(2,1)} %value_ref.7, bf16[1,384,4096]{2,1,0:T(8,128)(2,1)} %grad_ref.7, f32[64,384]{1,0:T(8,128)S(1)} %copy-done, ...), custom_call_target="tpu_custom_call" | custom-call | tf_op jit(solution)/shard_map/terms/pallas_call | solution.py:352
  151.2 4.0 %all-to-all-start.2 = ((f32[16,32,384]{2,1,0:T(8,128)}), f32[16,32,384]{2,1,0:T(8,128)S(1)}, u32[]{:S(2)}, u32[]{:S(2)}) async-start(f32[16,32,384]{2,1,0:T(8,128)} %terms.1), calls=%async_computation.2 | async-start | bytes 1572864 | tf_op jit(solution)/shard_map/all_to_all | solution.py:324
  155.2 12.7 %full.1 = (bf16[1,384,4096]{2,1,0:T(8,128)(2,1)}, bf16[1,384,4096]{2,1,0:T(8,128)(2,1)}, bf16[1,384,4096]{2,1,0:T(8,128)(2,1)}) custom-call(bf16[1,384,4096]{2,1,0:T(8,128)(2,1)} %key_ref.5, bf16[1,384,4096]{2,1,0:T(8,128)(2,1)} %value_ref.7, bf16[1,384,4096]{2,1,0:T(8,128)(2,1)} %grad_ref.7, f32[64,384]{1,0:T(8,128)S(1)} %copy-done, ...), custom_call_target="tpu_custom_call" | custom-call | tf_op jit(solution)/shard_map/full/pallas_call | solution.py:375
  167.9 0.0 all-to-all-done.2
  168.0 3.2 %collective-permute-start = (f32[32,384]{1,0:T(8,128)S(1)}, f32[32,384]{1,0:T(8,128)S(1)}, u32[]{:S(2)}, u32[]{:S(2)}) collective-permute-start(f32[32,384]{1,0:T(8,128)S(1)} %reduce_sum.9), channel_id=1, source_target_pairs={{0,16},{16,0},{32,48},{48,32},{64,80},{80,64},{96,112},{112,96},{1... | collective-permute-start | bytes 147464 | tf_op jit(solution)/shard_map/ppermute | solution.py:337
  171.1 0.9 collective-permute-done
  172.0 3.6 %collective-permute-start.1 = (f32[32,384]{1,0:T(8,128)S(1)}, f32[32,384]{1,0:T(8,128)S(1)}, u32[]{:S(2)}, u32[]{:S(2)}) collective-permute-start(f32[32,384]{1,0:T(8,128)S(1)} %add.12), channel_id=1, source_target_pairs={{0,64},{16,80},{32,96},{48,112},{64,0},{80,16},{96,32},{112,48},{1... | collective-permute-start | bytes 147464 | tf_op jit(solution)/shard_map/ppermute | solution.py:339
  175.7 0.7 collective-permute-start.2
  176.4 1.9 %collective-permute-start.3 = (f32[32,384]{1,0:T(8,128)S(1)}, f32[32,384]{1,0:T(8,128)S(1)}, u32[]{:S(2)}, u32[]{:S(2)}) collective-permute-start(f32[32,384]{1,0:T(8,128)S(1)} %add.12), channel_id=1, source_target_pairs={{0,96},{16,112},{32,0},{48,16},{64,32},{80,48},{96,64},{112,80},{1... | collective-permute-start | bytes 147464 | tf_op jit(solution)/shard_map/ppermute | solution.py:339
  178.3 0.0 collective-permute-done.1
  178.4 1.5 collective-permute-done.2
  179.8 0.0 collective-permute-done.3
  179.8 0.6 add_multiply_fusion
  (2 shorter events, 0.1 us)
Async XLA Ops:
  74.3 4.7 %copy-start.1 = (f32[32,384]{1,0:T(8,128)S(1)}, f32[32,384]{1,0:T(8,128)}, u32[]{:S(2)}) copy-start(f32[32,384]{1,0:T(8,128)} %get-tuple-element.20.running_ref) | copy-start | bytes 147460
  74.3 65.1 %all-to-all-start.1 = ((f32[16,520,128]{2,1,0:T(8,128)}), f32[16,520,128]{2,1,0:T(8,128)}, u32[]{:S(2)}, u32[]{:S(2)}) async-start(f32[16,520,128]{2,1,0:T(8,128)} %scan.1), calls=%async_computation.1 | async-start | bytes 8519680 | tf_op jit(solution)/shard_map/all_to_all | solution.py:324
  79.0 60.4 %copy-start = (f32[64,384]{1,0:T(8,128)S(1)}, f32[64,384]{1,0:T(8,128)}, u32[]{:S(2)}) copy-start(f32[64,384]{1,0:T(8,128)} %get-tuple-element.18.decay_ref) | copy-start | bytes 294916
  79.0 60.4 %copy-start.2 = (f32[32,384]{1,0:T(8,128)S(1)}, f32[32,384]{1,0:T(8,128)}, u32[]{:S(2)}) copy-start(f32[32,384]{1,0:T(8,128)} %get-tuple-element.30.slope_ref) | copy-start | bytes 147460
  151.2 16.7 %all-to-all-start.2 = ((f32[16,32,384]{2,1,0:T(8,128)}), f32[16,32,384]{2,1,0:T(8,128)S(1)}, u32[]{:S(2)}, u32[]{:S(2)}) async-start(f32[16,32,384]{2,1,0:T(8,128)} %terms.1), calls=%async_computation.2 | async-start | bytes 1572864 | tf_op jit(solution)/shard_map/all_to_all | solution.py:324
  168.0 4.1 %collective-permute-start = (f32[32,384]{1,0:T(8,128)S(1)}, f32[32,384]{1,0:T(8,128)S(1)}, u32[]{:S(2)}, u32[]{:S(2)}) collective-permute-start(f32[32,384]{1,0:T(8,128)S(1)} %reduce_sum.9), channel_id=1, source_target_pairs={{0,16},{16,0},{32,48},{48,32},{64,80},{80,64},{96,112},{112,96},{1... | collective-permute-start | bytes 147464 | tf_op jit(solution)/shard_map/ppermute | solution.py:337
  172.0 6.3 %collective-permute-start.1 = (f32[32,384]{1,0:T(8,128)S(1)}, f32[32,384]{1,0:T(8,128)S(1)}, u32[]{:S(2)}, u32[]{:S(2)}) collective-permute-start(f32[32,384]{1,0:T(8,128)S(1)} %add.12), channel_id=1, source_target_pairs={{0,64},{16,80},{32,96},{48,112},{64,0},{80,16},{96,32},{112,48},{1... | collective-permute-start | bytes 147464 | tf_op jit(solution)/shard_map/ppermute | solution.py:339
  175.7 4.2 %collective-permute-start.2 = (f32[32,384]{1,0:T(8,128)S(1)}, f32[32,384]{1,0:T(8,128)S(1)}, u32[]{:S(2)}, u32[]{:S(2)}) collective-permute-start(f32[32,384]{1,0:T(8,128)S(1)} %add.12), channel_id=1, source_target_pairs={{0,32},{16,48},{32,64},{48,80},{64,96},{80,112},{96,0},{112,16},{1... | collective-permute-start | bytes 147464 | tf_op jit(solution)/shard_map/ppermute | solution.py:339
  176.4 3.4 %collective-permute-start.3 = (f32[32,384]{1,0:T(8,128)S(1)}, f32[32,384]{1,0:T(8,128)S(1)}, u32[]{:S(2)}, u32[]{:S(2)}) collective-permute-start(f32[32,384]{1,0:T(8,128)S(1)} %add.12), channel_id=1, source_target_pairs={{0,96},{16,112},{32,0},{48,16},{64,32},{80,48},{96,64},{112,80},{1... | collective-permute-start | bytes 147464 | tf_op jit(solution)/shard_map/ppermute | solution.py:339

commit v5 on v3

--- a/solution.py
+++ b/solution.py
@@ -19,7 +19,7 @@
 GATE_STEPS = MODEL // GATE_STEP
 STATE_HEADS = 8
 LOCAL_HEADS = 2
-TERM_HEADS = 8
+TERM_HEADS = 16
 TERM_STEPS = HEADS // TERM_HEADS
 FULL_HEADS = 8
 TERM_OWNERS = 8

time: 181 us -> 181 us (level)
  no operation moved by 1% of the time
where the time goes in v5:
time: 181 us; the launch traced here: 179 us
  Pallas kernels  63.4 us (35%)
  blocking collectives  58.2 us (32%)
  waiting for transfers between devices  38.3 us (21%)
  starting transfers between devices  18.2 us (10%)
    all_to_all x1, blocking collectives, exchanged(): return lax.all_to_all(array, axis, 0, 0, tiled=True)  58.2 us
    all_to_all x2, waiting for transfers between devices, exchanged(): return lax.all_to_all(array, axis, 0, 0, tiled=True)  35.9 us
    pallas_call x1, Pallas kernels, locals_of(): pl.pallas_call(local_kernel, grid=(HEADS // LOCAL_HEADS,), in_specs=[head...  24.5 us
    pallas_call x1, Pallas kernels, full_of(): pl.pallas_call(full_kernel, grid=(HEADS // FULL_HEADS,), in_specs=[heads_...  12.7 us
    pallas_call x1, Pallas kernels, states_of(): pl.pallas_call(state_kernel, grid=(GATE_STEPS + HEADS // STATE_HEADS,), i...  12 us
    pallas_call x1, Pallas kernels, terms_of(): pl.pallas_call(term_kernel, grid=(TERM_STEPS + GROUPS // TERM_OWNERS,), i...  11.5 us
    all_to_all x2, starting transfers between devices, exchanged(): return lax.all_to_all(array, axis, 0, 0, tiled=True)  8.66 us
    ppermute x3, starting transfers between devices, summed_over_dp(): lax.ppermute(pair, 'dp', [(i, (i + 2 * step) % count) for i in range(coun...  6.31 us
  transfers between devices with their start and end apart: 6, of which 3 were waited for; matrix products, arithmetic and copies ran while one was open for 0% of the time, Pallas kernels for 21%

profile of v5, /device:TPU:1, one launch (start us, length us, event | category | flops | bytes accessed | tf_op | source)
XLA Modules:
  0.0 179.4 jit_solution(17165739343902086142)
XLA Ops:
  0.6 12.0 %states.1 = (f32[32,384]{1,0:T(8,128)}, f32[32,384]{1,0:T(8,128)}, f32[64,384]{1,0:T(8,128)}, f32[16,520,128]{2,1,0:T(8,128)}) custom-call(bf16[1,384,6144]{2,1,0:T(8,128)(2,1)} %input_ref.3, bf16[32,6144]{1,0:T(8,128)(2,1)} %bitcast.1, f32[1,32,384]{2,1,0:T(8,128)} %rate_ref.1, bf16[1,384,4096]{2,1,0:T(8,128)(2,1)} %query_ref.3, ...), custom_call_target="tpu_custom_call" | custom-call | tf_op jit(solution)/shard_map/states/pallas_call | solution.py:272
  12.6 58.2 %all_to_all.15.states_ref.rows_ref = f32[16,520,128]{2,1,0:T(8,128)S(1)} all-to-all(f32[16,520,128]{2,1,0:T(8,128)} %get-tuple-element.19), channel_id=1, replica_groups=mesh['dp'=8,'seq'=16] {'seq'}, dimensions={0} | all-to-all | bytes 8519680 | tf_op jit(solution)/shard_map/all_to_all | solution.py:327
  70.8 2.8 %scan.1 = f32[16,520,128]{2,1,0:T(8,128)} custom-call(f32[16,520,128]{2,1,0:T(8,128)S(1)} %all_to_all.15.states_ref.rows_ref, f32[16,520,128]{2,1,0:T(8,128)S(1)} %all_to_all.15.states_ref.rows_ref), custom_call_target="tpu_custom_call" | custom-call | tf_op jit(solution)/shard_map/scan/pallas_call | solution.py:311
  73.5 0.0 copy-start.1
  73.6 4.7 %all-to-all-start.1 = ((f32[16,520,128]{2,1,0:T(8,128)}), f32[16,520,128]{2,1,0:T(8,128)}, u32[]{:S(2)}, u32[]{:S(2)}) async-start(f32[16,520,128]{2,1,0:T(8,128)} %scan.1), calls=%async_computation.1 | async-start | bytes 8519680 | tf_op jit(solution)/shard_map/all_to_all | solution.py:327
  78.2 0.0 copy-done.1
  78.2 0.0 copy-start
  78.3 0.0 copy-start.2
  78.3 24.5 %locals.1 = (bf16[384,4096]{1,0:T(8,128)(2,1)}, bf16[384,4096]{1,0:T(8,128)(2,1)}, bf16[384,4096]{1,0:T(8,128)(2,1)}, bf16[4096,384]{1,0:T(8,128)(2,1)}, bf16[40...) custom-call(bf16[1,384,4096]{2,1,0:T(8,128)(2,1)} %query_ref.3, bf16[1,384,4096]{2,1,0:T(8,128)(2,1)} %key_ref.5, ...), custom_call_target="tpu_custom_call" | custom-call | tf_op jit(solution)/shard_map/locals/pallas_call | solution.py:292
  102.7 35.9 %all-to-all-done.1.carried_ref = f32[16,520,128]{2,1,0:T(8,128)} async-done(((f32[16,520,128]{2,1,0:T(8,128)}), f32[16,520,128]{2,1,0:T(8,128)}, u32[]{:S(2)}, u32[]{:S(2)}) %all-to-all-start.1) | async-done | bytes 4259872 | tf_op jit(solution)/shard_map/all_to_all | solution.py:327
  138.7 0.0 copy-done
  138.7 0.0 copy-done.2
  138.7 11.5 %terms.1 = f32[16,32,384]{2,1,0:T(8,128)} custom-call(bf16[4096,384]{1,0:T(8,128)(2,1)} %get-tuple-element.27.query_ref, bf16[4096,384]{1,0:T(8,128)(2,1)} %get-tuple-element.28.key_ref, bf16[1,384,4096]{2,1,0:T(8,128)(2,1)} %value_ref.7, bf16[1,384,4096]{2,1,0:T(8,128)(2,1)} %grad_ref.7, f32[64,384]{1,0:T(8,128)S(1)} %copy-done, ...), custom_call_target="tpu_custom_call" | custom-call | tf_op jit(solution)/shard_map/terms/pallas_call | solution.py:355
  150.2 4.0 %all-to-all-start.2 = ((f32[16,32,384]{2,1,0:T(8,128)}), f32[16,32,384]{2,1,0:T(8,128)S(1)}, u32[]{:S(2)}, u32[]{:S(2)}) async-start(f32[16,32,384]{2,1,0:T(8,128)} %terms.1), calls=%async_computation.2 | async-start | bytes 1572864 | tf_op jit(solution)/shard_map/all_to_all | solution.py:327
  154.1 12.7 %full.1 = (bf16[1,384,4096]{2,1,0:T(8,128)(2,1)}, bf16[1,384,4096]{2,1,0:T(8,128)(2,1)}, bf16[1,384,4096]{2,1,0:T(8,128)(2,1)}) custom-call(bf16[1,384,4096]{2,1,0:T(8,128)(2,1)} %key_ref.5, bf16[1,384,4096]{2,1,0:T(8,128)(2,1)} %value_ref.7, bf16[1,384,4096]{2,1,0:T(8,128)(2,1)} %grad_ref.7, f32[64,384]{1,0:T(8,128)S(1)} %copy-done, ...), custom_call_target="tpu_custom_call" | custom-call | tf_op jit(solution)/shard_map/full/pallas_call | solution.py:378
  166.9 0.0 all-to-all-done.2
  167.0 3.2 %collective-permute-start = (f32[32,384]{1,0:T(8,128)S(1)}, f32[32,384]{1,0:T(8,128)S(1)}, u32[]{:S(2)}, u32[]{:S(2)}) collective-permute-start(f32[32,384]{1,0:T(8,128)S(1)} %reduce_sum.9), channel_id=1, source_target_pairs={{0,16},{16,0},{32,48},{48,32},{64,80},{80,64},{96,112},{112,96},{1... | collective-permute-start | bytes 147464 | tf_op jit(solution)/shard_map/ppermute | solution.py:340
  170.1 0.9 collective-permute-done
  171.0 3.6 %collective-permute-start.1 = (f32[32,384]{1,0:T(8,128)S(1)}, f32[32,384]{1,0:T(8,128)S(1)}, u32[]{:S(2)}, u32[]{:S(2)}) collective-permute-start(f32[32,384]{1,0:T(8,128)S(1)} %add.12), channel_id=1, source_target_pairs={{0,64},{16,80},{32,96},{48,112},{64,0},{80,16},{96,32},{112,48},{1... | collective-permute-start | bytes 147464 | tf_op jit(solution)/shard_map/ppermute | solution.py:342
  174.7 0.7 collective-permute-start.2
  175.4 1.9 %collective-permute-start.3 = (f32[32,384]{1,0:T(8,128)S(1)}, f32[32,384]{1,0:T(8,128)S(1)}, u32[]{:S(2)}, u32[]{:S(2)}) collective-permute-start(f32[32,384]{1,0:T(8,128)S(1)} %add.12), channel_id=1, source_target_pairs={{0,96},{16,112},{32,0},{48,16},{64,32},{80,48},{96,64},{112,80},{1... | collective-permute-start | bytes 147464 | tf_op jit(solution)/shard_map/ppermute | solution.py:342
  177.3 0.0 collective-permute-done.1
  177.3 1.5 collective-permute-done.2
  178.8 0.0 collective-permute-done.3
  178.8 0.6 add_multiply_fusion
  (2 shorter events, 0.1 us)
Async XLA Ops:
  73.5 4.7 %copy-start.1 = (f32[32,384]{1,0:T(8,128)S(1)}, f32[32,384]{1,0:T(8,128)}, u32[]{:S(2)}) copy-start(f32[32,384]{1,0:T(8,128)} %get-tuple-element.20.running_ref) | copy-start | bytes 147460
  73.6 65.1 %all-to-all-start.1 = ((f32[16,520,128]{2,1,0:T(8,128)}), f32[16,520,128]{2,1,0:T(8,128)}, u32[]{:S(2)}, u32[]{:S(2)}) async-start(f32[16,520,128]{2,1,0:T(8,128)} %scan.1), calls=%async_computation.1 | async-start | bytes 8519680 | tf_op jit(solution)/shard_map/all_to_all | solution.py:327
  78.2 60.4 %copy-start = (f32[64,384]{1,0:T(8,128)S(1)}, f32[64,384]{1,0:T(8,128)}, u32[]{:S(2)}) copy-start(f32[64,384]{1,0:T(8,128)} %get-tuple-element.18.decay_ref) | copy-start | bytes 294916
  78.3 60.4 %copy-start.2 = (f32[32,384]{1,0:T(8,128)S(1)}, f32[32,384]{1,0:T(8,128)}, u32[]{:S(2)}) copy-start(f32[32,384]{1,0:T(8,128)} %get-tuple-element.30.slope_ref) | copy-start | bytes 147460
  150.2 16.7 %all-to-all-start.2 = ((f32[16,32,384]{2,1,0:T(8,128)}), f32[16,32,384]{2,1,0:T(8,128)S(1)}, u32[]{:S(2)}, u32[]{:S(2)}) async-start(f32[16,32,384]{2,1,0:T(8,128)} %terms.1), calls=%async_computation.2 | async-start | bytes 1572864 | tf_op jit(solution)/shard_map/all_to_all | solution.py:327
  167.0 4.1 %collective-permute-start = (f32[32,384]{1,0:T(8,128)S(1)}, f32[32,384]{1,0:T(8,128)S(1)}, u32[]{:S(2)}, u32[]{:S(2)}) collective-permute-start(f32[32,384]{1,0:T(8,128)S(1)} %reduce_sum.9), channel_id=1, source_target_pairs={{0,16},{16,0},{32,48},{48,32},{64,80},{80,64},{96,112},{112,96},{1... | collective-permute-start | bytes 147464 | tf_op jit(solution)/shard_map/ppermute | solution.py:340
  171.0 6.3 %collective-permute-start.1 = (f32[32,384]{1,0:T(8,128)S(1)}, f32[32,384]{1,0:T(8,128)S(1)}, u32[]{:S(2)}, u32[]{:S(2)}) collective-permute-start(f32[32,384]{1,0:T(8,128)S(1)} %add.12), channel_id=1, source_target_pairs={{0,64},{16,80},{32,96},{48,112},{64,0},{80,16},{96,32},{112,48},{1... | collective-permute-start | bytes 147464 | tf_op jit(solution)/shard_map/ppermute | solution.py:342
  174.7 4.2 %collective-permute-start.2 = (f32[32,384]{1,0:T(8,128)S(1)}, f32[32,384]{1,0:T(8,128)S(1)}, u32[]{:S(2)}, u32[]{:S(2)}) collective-permute-start(f32[32,384]{1,0:T(8,128)S(1)} %add.12), channel_id=1, source_target_pairs={{0,32},{16,48},{32,64},{48,80},{64,96},{80,112},{96,0},{112,16},{1... | collective-permute-start | bytes 147464 | tf_op jit(solution)/shard_map/ppermute | solution.py:342
  175.4 3.4 %collective-permute-start.3 = (f32[32,384]{1,0:T(8,128)S(1)}, f32[32,384]{1,0:T(8,128)S(1)}, u32[]{:S(2)}, u32[]{:S(2)}) collective-permute-start(f32[32,384]{1,0:T(8,128)S(1)} %add.12), channel_id=1, source_target_pairs={{0,96},{16,112},{32,0},{48,16},{64,32},{80,48},{96,64},{112,80},{1... | collective-permute-start | bytes 147464 | tf_op jit(solution)/shard_map/ppermute | solution.py:342
